TPU v7x, 256 devices: a whole 4x4x8 slice. The times are simulated.
256 devices in a mesh: group: 16 (over z, core), tensor: 4 (over x), seq: 4 (over y).
Axes of the slice: x: 4, y: 4, z: 8, core: 2. Of those that a mesh axis runs over, the one named last changes fastest.
Arguments:
- hidden: bfloat16 [4096, 8192], P('group', ('tensor', 'seq')), may hold values from -6 to 6
- key_value_weight: bfloat16 [8192, 8, 2, 128], P(('tensor', 'seq')), may hold values from -0.0625 to 0.0625
- adapter_down_weight: bfloat16 [64, 8192, 128], P('group', ('tensor', 'seq')), may hold values from -0.0625 to 0.0625
- adapter_up_weight: bfloat16 [64, 2, 64, 1024], P('group', None, None, 'tensor'), may hold values from -0.75 to 0.75
- queries: bfloat16 [4096, 8192], P('group', 'tensor'), may hold values from -120 to 120
- key_value_cache: bfloat16 [32, 16384, 8, 2, 128], P('group', 'seq', 'tensor'), may hold values from -6.08 to 6.08
- request_adapter: int32 [32], replicated, may hold values from 0 to 63
Outputs:
- new_kv: bfloat16 [4096, 8, 2, 128], P(('group', 'seq'), 'tensor')
- attention: bfloat16 [4096, 8192], P(('group', 'seq'), 'tensor')
All inputs are finite; a program needn't handle non-finite values.
Results may differ from a plain program's by a relative error of at most 0.012.
Values may be sent and summed in bfloat16 or wider, within the bound.
No kernel may reach another device: no remote copies, remote signals or barrier semaphores. Data moves between devices by JAX's collectives and lax.ppermute only.
A program may use at most 192 MiB of HBM per device.

v0:
```python
import math

import jax
import jax.numpy as jnp
from jax import lax
from jax.sharding import PartitionSpec as P

HEADS = 64
KEY_VALUE_HEADS = 8
NEW_TOK = 128
CACHE = 16384


def merged_2(shard, axis, combine):
    everything = jax.tree.map(lambda part: lax.all_gather(part, axis), shard)
    leading = jax.tree.map(lambda part: part[0], everything)

    def turn(k, so_far):
        return combine(so_far, jax.tree.map(lambda part: part[k], everything))

    return lax.fori_loop(1, lax.axis_size(axis), turn, leading)


def rotate(field, positions):
    half_dim = field.shape[-1] // 2
    exponents = jnp.arange(half_dim, dtype=jnp.float32)
    frequency = jnp.exp(exponents * (-2.0 * math.log(500000.0) / field.shape[-1]))
    angles = positions.astype(jnp.float32)[:, None, None] * frequency[None, None, :]
    cos_table = jnp.cos(angles)
    sin_table = jnp.sin(angles)
    upper_half = field[..., :half_dim]
    lower_half = field[..., half_dim:]
    return jnp.concatenate(
        [
            upper_half * cos_table - lower_half * sin_table,
            lower_half * cos_table + upper_half * sin_table,
        ],
        axis=-1,
    )


def choose_rows(selected, block, needed_rows):
    hit_mask = (
        needed_rows[:, None] == jnp.arange(block.shape[0], dtype=jnp.int32)[None, :]
    ).astype(block.dtype)
    flat_block = block.reshape(block.shape[0], -1)
    picked = jnp.dot(hit_mask, flat_block, preferred_element_type=jnp.float32)
    return picked.reshape(selected.shape)


def local(
    hidden,
    key_value_weight,
    adapter_down_weight,
    adapter_up_weight,
    queries,
    key_value_cache,
    request_adapter,
):
    tensor_count = lax.axis_size("tensor")
    seq_count = lax.axis_size("seq")
    seq_index = lax.axis_index("seq")
    group_index = lax.axis_index("group")
    token_count = hidden.shape[0]
    slice_width = hidden.shape[1]
    request_own_rows = token_count // seq_count
    request_total = token_count // NEW_TOK
    shard_heads = key_value_cache.shape[2]
    head_size_value = key_value_cache.shape[4]
    rank_size_value = adapter_down_weight.shape[2]
    group_size = HEADS // KEY_VALUE_HEADS
    weight_cols = key_value_weight.reshape(
        slice_width, tensor_count, shard_heads * 2 * head_size_value
    )

    def one_block(block_id):
        tokens_here = lax.dynamic_slice_in_dim(
            hidden, block_id % seq_count * request_own_rows, request_own_rows, 0
        )
        cols_here = lax.dynamic_index_in_dim(weight_cols, block_id // seq_count, 1, keepdims=False)
        return jnp.dot(tokens_here, cols_here, preferred_element_type=jnp.float32)

    block_ids = jnp.arange(
        lax.axis_size(("tensor", "seq")) * request_own_rows // request_own_rows, dtype=jnp.int32
    )
    base_key_value = lax.psum_scatter(
        lax.map(one_block, block_ids).reshape(
            lax.axis_size(("tensor", "seq")) * request_own_rows, shard_heads, 2, head_size_value
        ),
        ("tensor", "seq"),
        scatter_dimension=0,
        tiled=True,
    )
    needed_rows = lax.dynamic_slice_in_dim(
        request_adapter, group_index * request_total, request_total, 0
    )
    zero_up_weight = jnp.zeros((request_total,) + adapter_up_weight.shape[1:], jnp.float32)
    zero_down_weight = jnp.zeros((request_total,) + adapter_down_weight.shape[1:], jnp.float32)
    down_float = choose_rows(
        zero_down_weight,
        lax.all_gather(adapter_down_weight, "group", axis=0, tiled=True),
        needed_rows,
    )
    up_weight_float = choose_rows(
        zero_up_weight, lax.all_gather(adapter_up_weight, "group", axis=0, tiled=True), needed_rows
    )
    down_pick = down_float.astype(jnp.bfloat16)
    up_pick = up_weight_float.astype(jnp.bfloat16)
    partial_rank = jnp.einsum(
        "rtd,rdk->rtk",
        hidden.reshape(request_total, NEW_TOK, slice_width),
        down_pick,
        preferred_element_type=jnp.float32,
    )
    rank_part = lax.psum_scatter(
        partial_rank.reshape(token_count, rank_size_value), "seq", scatter_dimension=0, tiled=True
    )
    rank_vec = lax.psum(rank_part, "tensor").astype(jnp.bfloat16)
    local_rows = seq_index * request_own_rows + jnp.arange(request_own_rows, dtype=jnp.int32)
    local_request = local_rows // NEW_TOK
    token_pos = local_rows % NEW_TOK
    all_adapter_deltas = jnp.einsum(
        "oej,rejc->roec",
        rank_vec.reshape(request_own_rows, 2, rank_size_value // 2),
        up_pick,
        preferred_element_type=jnp.float32,
    )
    request_row_mask = (
        jnp.arange(request_total, dtype=jnp.int32)[:, None] == local_request[None, :]
    ).astype(jnp.float32)
    adapter_delta = jnp.sum(request_row_mask[:, :, None, None] * all_adapter_deltas, axis=0)
    adapter_delta = adapter_delta.reshape(
        request_own_rows, 2, shard_heads, head_size_value
    ).transpose(0, 2, 1, 3)
    delta_sum = base_key_value + adapter_delta
    rotated = rotate(delta_sum[:, :, 0, :], CACHE + token_pos)
    new_kv = jnp.stack([rotated, delta_sum[:, :, 1, :]], axis=2).astype(jnp.bfloat16)
    score_scale = 1.0 / math.sqrt(head_size_value)
    query_all = queries.reshape(request_total, NEW_TOK, shard_heads, group_size, head_size_value)
    new_keys = new_kv[:, :, 0, :]
    new_values = new_kv[:, :, 1, :]
    query_pos = jnp.arange(NEW_TOK, dtype=jnp.int32)
    top_list = []
    total_list = []
    value_list = []
    for request in range(request_total):
        query_rows = query_all[request]
        cache_rows = key_value_cache[request]
        old_scores = (
            jnp.einsum(
                "qgjh,pgh->qgjp",
                query_rows,
                cache_rows[:, :, 0],
                preferred_element_type=jnp.float32,
            )
            * score_scale
        )
        new_scores = (
            jnp.einsum("qgjh,ugh->qgju", query_rows, new_keys, preferred_element_type=jnp.float32)
            * score_scale
        )
        allowed = (local_request[None, :] == request) & (token_pos[None, :] <= query_pos[:, None])
        new_scores = jnp.where(allowed[:, None, None, :], new_scores, -1e30)
        row_top = jnp.maximum(old_scores.max(-1), new_scores.max(-1))
        old_exp = jnp.exp(old_scores - row_top[..., None])
        new_exp = jnp.exp(new_scores - row_top[..., None])
        top_list.append(row_top)
        total_list.append(old_exp.sum(-1) + new_exp.sum(-1))
        value_sum = jnp.einsum(
            "qgjp,pgh->qgjh",
            old_exp.astype(jnp.bfloat16),
            cache_rows[:, :, 1],
            preferred_element_type=jnp.float32,
        )
        value_sum = value_sum + jnp.einsum(
            "qgju,ugh->qgjh",
            new_exp.astype(jnp.bfloat16),
            new_values,
            preferred_element_type=jnp.float32,
        )
        value_list.append(value_sum)
    top_all = jnp.stack(top_list).reshape(token_count, shard_heads, group_size)
    total_all = jnp.stack(total_list).reshape(token_count, shard_heads, group_size)
    value_all = jnp.stack(value_list).reshape(token_count, shard_heads, group_size, head_size_value)

    def combine(earlier, later):
        joined_top = jnp.maximum(earlier[0], later[0])
        earlier_scale = jnp.exp(earlier[0] - joined_top)
        later_scale = jnp.exp(later[0] - joined_top)
        return (
            joined_top,
            earlier[1] * earlier_scale + later[1] * later_scale,
            earlier[2] * earlier_scale[..., None] + later[2] * later_scale[..., None],
        )

    merged = merged_2((top_all, total_all, value_all), "seq", combine)
    total_own = lax.dynamic_slice_in_dim(
        merged[1], seq_index * request_own_rows, request_own_rows, 0
    )
    value_own = lax.dynamic_slice_in_dim(
        merged[2], seq_index * request_own_rows, request_own_rows, 0
    )
    attention = (
        (value_own / total_own[..., None])
        .reshape(request_own_rows, shard_heads * group_size * head_size_value)
        .astype(jnp.bfloat16)
    )
    return (new_kv, attention)


def solution(mesh):
    in_specs = (
        P("group", ("tensor", "seq")),
        P(("tensor", "seq"), None, None, None),
        P("group", ("tensor", "seq"), None),
        P("group", None, None, "tensor"),
        P("group", "tensor"),
        P("group", "seq", "tensor", None, None),
        P(),
    )
    out_specs = (P(("group", "seq"), "tensor", None, None), P(("group", "seq"), "tensor"))
    return jax.shard_map(local, mesh=mesh, in_specs=in_specs, out_specs=out_specs, check_vma=False)
```

profile of v0, /device:TPU:32, one launch (start us, length us, event | category | flops | bytes accessed | tf_op | source)
XLA Modules:
  0.0 375.2 jit_solution(4002112408915859827)
XLA Ops:
  7.2 0.7 all-gather.6.cloned.1.call-update
  8.0 0.7 all-gather.4.cloned.1.call-update
  8.7 4.7 %copy.87 = bf16[512,8,2,128]{0,3,2,1:T(8,128)(2,1)S(1)} copy(bf16[512,8,2,128]{3,2,1,0:T(2,128)(2,1)} %param.12) | data formatting | bytes 4194304 | tf_op args[1]
  13.5 53.0 %all-gather.6.cloned.1.call-done = bf16[64,512,128]{2,1,0:T(8,128)(2,1)} async-done(((bf16[4,512,128]{2,1,0:T(8,128)(2,1)}), bf16[64,512,128]{2,1,0:T(8,128)(2,1)}) %all-gather.6.cloned.1.call-update) | async-done | bytes 8388624 | tf_op jit(solution)/shard_map/all_gather | solution.py:101
  66.6 8.0 %fusion.39 = bf16[2,512,128]{2,0,1:T(2,128)(2,1)S(1)} fusion(s32[2]{0:T(128)S(1)} %dynamic_slice.59, bf16[8,8,512,128]{3,2,1,0:T(8,128)(2,1)} %bitcast.240), kind=kOutput, calls=%fused_computation.56 | convolution fusion | flops 16908416 | bytes 8650760 | tf_op jit(solution)/shard_map/dot_general | solution.py:47
  74.6 0.9 fusion.52
  75.6 70.4 %while.31 = (s32[]{:T(128)}, f32[16,64,512]{2,1,0:T(8,128)}, s32[16]{0:T(128)S(1)}, bf16[256,512]{1,0:T(8,128)(2,1)S(1)}, bf16[512,4,512]{0,2,1:T(8,128)(2,1)S(1...) while((s32[]{:T(128)}, f32[16,64,512]{2,1,0:T(8,128)}, ...), condition=%wide.region_1.2_spmd, body=%wide.region_0.1_spmd.sunk | while | flops 33554460 | bytes 721320 | solution.py:87
  75.6 0.7 dynamic_slice.83
  79.0 0.9 fusion.92
  80.0 0.7 dynamic_slice.83
  83.4 0.9 fusion.92
  84.4 0.7 dynamic_slice.83
  87.8 0.9 fusion.92
  88.8 0.7 dynamic_slice.83
  92.2 0.9 fusion.92
  93.2 0.7 dynamic_slice.83
  96.6 0.9 fusion.92
  97.6 0.7 dynamic_slice.83
  101.0 0.9 fusion.92
  102.0 0.7 dynamic_slice.83
  105.4 0.9 fusion.92
  106.4 0.7 dynamic_slice.83
  109.8 0.9 fusion.92
  110.8 0.7 dynamic_slice.83
  114.2 0.9 fusion.92
  115.2 0.7 dynamic_slice.83
  118.6 0.9 fusion.92
  119.6 0.7 dynamic_slice.83
  123.0 0.9 fusion.92
  124.0 0.7 dynamic_slice.83
  127.4 0.9 fusion.92
  128.4 0.7 dynamic_slice.83
  131.8 0.9 fusion.92
  132.8 0.7 dynamic_slice.83
  136.2 0.9 fusion.92
  140.6 0.9 fusion.92
  145.0 0.9 fusion.92
  146.0 2.6 reshape.299
  148.6 1.5 copy.89
  151.1 7.1 %fusion.73 = (bf16[1,4096,2,2,128]{4,3,2,1,0:T(2,128)(2,1)S(1)}, bf16[1,4096,2,2,128]{4,3,2,1,0:T(2,128)(2,1)S(1)}) fusion(bf16[2,4096,2,2,128]{4,3,2,1,0:T(2,128)(2,1)} %param.16), kind=kLoop, calls=%fused_computation.118 | loop fusion | bytes 16777216 | tf_op jit(solution)/shard_map/slice | solution.py:148
  158.4 2.2 copy_bitcast_fusion
  160.8 13.2 %bitcast_reduce_fusion = (f32[128,2,8]{0,2,1:T(8,128)S(1)}, f32[2,4096,128,8]{2,1,3,0:T(8,128)}) fusion(bf16[128,2,8,128]{0,3,2,1:T(8,128)(2,1)S(1)} %bitcast.228, bf16[4096,2,2,128]{3,0,1,2:T(8,128)(2,1)S(1)} %get-tuple-element.325), kind=kOutput, calls=%fused_computation.15 | convolution fusion | flops 2164258816 | bytes 36184064 | tf_op jit(solution)/shard_map/qgjh,pgh->qgjp/dot_general | solution.py:150
  174.0 13.3 %bitcast_reduce_fusion.1 = (f32[128,2,8]{0,2,1:T(8,128)S(1)}, f32[2,4096,128,8]{2,1,3,0:T(8,128)}) fusion(bf16[128,2,8,128]{0,3,2,1:T(8,128)(2,1)S(1)} %bitcast.230, bf16[4096,2,2,128]{3,0,1,2:T(8,128)(2,1)S(1)} %get-tuple-element.326), kind=kOutput, calls=%fused_computation.18 | convolution fusion | flops 2164258816 | bytes 36184064 | tf_op jit(solution)/shard_map/qgjh,pgh->qgjp/dot_general | solution.py:150
  187.3 4.6 %fusion.43 = bf16[2,2,64,256]{3,0,2,1:T(2,128)(2,1)S(1)} fusion(bf16[2,64,256,64]{2,1,0,3:T(8,128)(2,1)} %bitcast.232, s32[2]{0:T(128)S(1)} %dynamic_slice.59), kind=kOutput, calls=%fused_computation.59 | convolution fusion | flops 8454272 | bytes 4325384 | tf_op jit(solution)/shard_map/dot_general | solution.py:47
  191.8 17.7 %psum.7 = bf16[64,128]{1,0:T(8,128)(2,1)S(1)} all-reduce(f32[64,128]{1,0:T(8,128)} %reduce-scatter.5.cloned.1.call-done), channel_id=1, replica_groups=mesh['group'=16,'tensor'=4,'seq'=4] {'tensor'}, use_global_device_ids=true, to_apply=%region_4.5 | all-reduce | flops 8192 | bytes 49152 | tf_op jit(solution)/shard_map/psum | solution.py:118
  209.8 20.3 %reduce-scatter.3.cloned.1.call-done = f32[64,2,2,128]{3,0,1,2:T(8,128)} async-done(((f32[1024,2,2,128]{3,0,1,2:T(8,128)}), f32[64,2,2,128]{3,0,1,2:T(8,128)}) %reduce-scatter.3.cloned.1.call-update) | async-done | bytes 131088 | tf_op jit(solution)/shard_map/reduce_scatter | solution.py:86
  230.1 0.9 fusion.56
  231.7 15.2 %fusion.32 = f32[128,2,8,128]{3,0,2,1:T(8,128)S(1)} fusion(bf16[4096,2,2,128]{3,0,1,2:T(8,128)(2,1)} %copy-done.1, f32[2,4096,128,8]{2,1,3,0:T(8,128)} %get-tuple-element.314, f32[128,2,8]{0,2,1:T(8,128)S(1)} %max.46), kind=kOutput, calls=%fused_computation.49 | convolution fusion | flops 2172649472 | bytes 36708352 | tf_op jit(solution)/shard_map/qgjp,pgh->qgjh/dot_general | solution.py:169
  246.9 1.3 fusion.28
  248.3 15.2 %fusion.29 = f32[128,2,8,128]{3,0,2,1:T(8,128)S(1)} fusion(bf16[4096,2,2,128]{3,0,1,2:T(8,128)(2,1)} %copy-done, f32[2,4096,128,8]{2,1,3,0:T(8,128)} %get-tuple-element.318, f32[128,2,8]{0,2,1:T(8,128)S(1)} %max.44), kind=kOutput, calls=%fused_computation.48 | convolution fusion | flops 2172649472 | bytes 36708352 | tf_op jit(solution)/shard_map/qgjp,pgh->qgjh/dot_general | solution.py:169
  263.8 1.4 pad_maximum_fusion
  265.2 2.6 copy.107
  267.9 0.7 copy.109
  268.6 12.1 %all_gather.17 = f32[4,256,2,8]{1,3,2,0:T(8,128)S(1)} all-gather(f32[1,256,2,8]{1,3,2,0:T(8,128)S(1)} %copy_bitcast_fusion.3), channel_id=1, replica_groups=mesh['group'=16,'tensor'=4,'seq'=4] {'seq'}, dimensions={0}, use_global_device_ids=true | all-gather | bytes 81920 | tf_op jit(solution)/shard_map/all_gather | solution.py:15
  281.0 14.4 %fusion.13 = f32[128,2,8]{0,2,1:T(8,128)S(1)} fusion(f32[2,4096,128,8]{2,1,3,0:T(8,128)} %get-tuple-element.314, f32[128,2,8]{0,2,1:T(8,128)S(1)} %max.46), kind=kLoop, calls=%fused_computation.23 | loop fusion | flops 25163776 | bytes 33570816 | tf_op jit(solution)/shard_map/reduce_sum | solution.py:168
  295.4 13.7 %fusion.11 = f32[128,2,8]{0,2,1:T(8,128)S(1)} fusion(f32[2,4096,128,8]{2,1,3,0:T(8,128)} %get-tuple-element.318, f32[128,2,8]{0,2,1:T(8,128)S(1)} %max.44), kind=kLoop, calls=%fused_computation.21 | loop fusion | flops 25163776 | bytes 33570816 | tf_op jit(solution)/shard_map/reduce_sum | solution.py:168
  309.1 12.1 %all_gather.18 = f32[4,256,2,8]{1,3,2,0:T(8,128)S(1)} all-gather(f32[1,256,2,8]{1,3,2,0:T(8,128)S(1)} %maximum_bitcast_fusion), channel_id=1, replica_groups=mesh['group'=16,'tensor'=4,'seq'=4] {'seq'}, dimensions={0}, use_global_device_ids=true | all-gather | bytes 81920 | tf_op jit(solution)/shard_map/all_gather | solution.py:15
  321.2 32.3 %all-gather.8.cloned.1.call-done = f32[4,256,2,8,128]{4,3,2,1,0:T(8,128)} async-done(((f32[1,256,2,8,128]{4,3,2,1,0:T(8,128)}), f32[4,256,2,8,128]{4,3,2,1,0:T(8,128)}) %all-gather.8.cloned.1.call-update) | async-done | bytes 8388624 | tf_op jit(solution)/shard_map/all_gather | solution.py:15
  353.5 1.7 slice_bitcast_fusion
  355.3 12.2 %while.32 = (s32[]{:T(128)}, f32[256,2,8]{0,2,1:T(8,128)S(1)}, f32[256,2,8]{0,2,1:T(8,128)S(1)}, f32[256,2,8,128]{3,2,1,0:T(8,128)S(1)}, f32[4,256,2,8]{1,3,2,0:...) while((s32[]{:T(128)}, f32[256,2,8]{0,2,1:T(8,128)S(1)}, ...), condition=%wide.region_15.16_spmd, body=%wide.region_14.15_spmd.sunk | while | flops 1597445 | bytes 6520975 | solution.py:21
  355.7 3.7 fusion.94
  359.7 3.7 fusion.94
  363.8 3.7 fusion.94
  367.9 0.8 copy.161
  (67 shorter events, 5.9 us)
Async XLA Ops:
  7.2 6.3 %copy-start.4 = (s32[32]{0:T(128)S(1)}, s32[32]{0:T(128)}, u32[]{:S(2)}) copy-start(s32[32]{0:T(128)} %param.17) | copy-start | bytes 388
  7.2 59.4 %all-gather.6.cloned.1.call-start = ((), (), s32[]{:S(2)}) async-start(), calls=%async_computation.4 | async-start | bytes 8912896 | tf_op jit(solution)/shard_map/all_gather | solution.py:101
  7.9 179.4 %all-gather.4.cloned.1.call-start = ((), (), s32[]{:S(2)}) async-start(), calls=%async_computation.3 | async-start | bytes 4456448 | tf_op jit(solution)/shard_map/all_gather | solution.py:105
  8.7 183.2 %reduce-scatter.5.cloned.1.call-start = ((), (), s32[]{:S(2)}) async-start(), calls=%async_computation.5 | async-start | bytes 163840 | tf_op jit(solution)/shard_map/reduce_scatter | solution.py:115
  66.6 8.0 %copy-start.2 = (bf16[256,512]{1,0:T(8,128)(2,1)S(1)}, bf16[256,512]{1,0:T(8,128)(2,1)}, u32[]{:S(2)}) copy-start(bf16[256,512]{1,0:T(8,128)(2,1)} %param.11) | copy-start | bytes 786436
  75.5 154.6 %reduce-scatter.3.cloned.1.call-start = ((), (), s32[]{:S(2)}) async-start(), calls=%async_computation.2 | async-start | bytes 2228224 | tf_op jit(solution)/shard_map/reduce_scatter | solution.py:86
  148.6 1.9 copy-start.3
  150.1 203.4 %all-gather.8.cloned.1.call-start = ((), (), s32[]{:S(2)}) async-start(), calls=%async_computation.6 | async-start | bytes 10485760 | tf_op jit(solution)/shard_map/all_gather | solution.py:15
  160.7 13.3 %copy-start.1 = (bf16[4096,2,2,128]{3,0,1,2:T(8,128)(2,1)}, bf16[4096,2,2,128]{3,0,1,2:T(8,128)(2,1)S(1)}, u32[]{:S(2)}) copy-start(bf16[4096,2,2,128]{3,0,1,2:T(8,128)(2,1)S(1)} %get-tuple-element.325) | copy-start | bytes 12582916
  160.7 13.3 %copy-start = (bf16[4096,2,2,128]{3,0,1,2:T(8,128)(2,1)}, bf16[4096,2,2,128]{3,0,1,2:T(8,128)(2,1)S(1)}, u32[]{:S(2)}) copy-start(bf16[4096,2,2,128]{3,0,1,2:T(8,128)(2,1)S(1)} %get-tuple-element.326) | copy-start | bytes 12582916
Sparse Core Ops, SparseCore 0:
  9.8 56.6 all-gather.5
  68.4 42.4 all-gather.3
  114.0 21.7 reduce-scatter.4
  150.2 79.8 reduce-scatter.2
  267.9 85.5 all-gather.7
where the time goes:
time: 378 us; the launch traced here: 375 us
  waiting for transfers between devices  107 us (28%)
  matrix products  87.8 us (23%)
  loops' own time  44.9 us (12%)
  other arithmetic  42.5 us (11%)
  blocking collectives  41.9 us (11%)
  local copies, waits for them, and re-layouts  36.5 us (10%)
  between operations  14.1 us (4%)
    all_gather x1, waiting for transfers between devices, local(): lax.all_gather(adapter_down_weight, 'group', axis=0, tiled=True)  53 us
    another operation x1, loops' own time, local(): lax.map(one_block, block_ids)  44.7 us
    all_gather x1, waiting for transfers between devices, merged_2(): everything = jax.tree.map(lambda part: lax.all_gather(part, axis), shard)  32.3 us
    dot_general x2, matrix products, local(): jnp.einsum('qgjp,pgh->qgjh', old_exp.astype(jnp.bfloat16), cache_rows[:,...  30.3 us
    reduce_sum x4, other arithmetic, local(): total_list.append(old_exp.sum(-1) + new_exp.sum(-1))  28.3 us
    dot_general x2, matrix products, local(): jnp.einsum('qgjh,pgh->qgjp', query_rows, cache_rows[:, :, 0], preferred_e...  26.5 us
    all_gather x2, blocking collectives, merged_2(): everything = jax.tree.map(lambda part: lax.all_gather(part, axis), shard)  24.2 us
    reduce_scatter x1, waiting for transfers between devices, local(): lax.psum_scatter(lax.map(one_block, block_ids).reshape(lax.axis_size(('te...  20.3 us
  transfers between devices with their start and end apart: 5, of which 3 were waited for; matrix products, arithmetic and copies ran while one was open for 30% of the time, Pallas kernels for 0%

commit v1 on v0

v1 whole, which is shorter than its diff:
```python
import functools
import math

import jax
import jax.numpy as jnp
from jax import lax
from jax.experimental import pallas as pl
from jax.experimental.pallas import tpu as pltpu
from jax.sharding import PartitionSpec as P

NEW_TOK = 128
CACHE = 16384
WIDTH = 128
SCALE = math.log2(math.e) / math.sqrt(WIDTH)
KEY_BLOCK = 1024
TILE = 256
LOW = -1e30
BF = jnp.bfloat16
F32 = jnp.float32
VMEM_LIMIT = 56 * 2**20

SEQ, HALF, PARITY, TENSOR = 0, 1, 2, 3
ROW_OWN, HAS_OWN, ROW_MATE, HAS_MATE = 4, 6, 8, 10


def prep_kernel(where, hidden_ref, weight_ref, *rest):
    outs, wide = rest[:4], rest[4]
    wide[...] = weight_ref[...].astype(F32)
    depth = hidden_ref.shape[1]
    hidden = hidden_ref[...]
    for shift in range(4):
        dest = lax.rem(where[TENSOR] + shift, 4)
        cols = [
            wide[pl.ds(dest * 4 + part, depth, stride=16), :].astype(BF) for part in range(4)
        ]
        rhs = jnp.concatenate(cols, axis=1)
        outs[shift][...] = jnp.dot(hidden, rhs, preferred_element_type=F32).astype(BF)


def prep(where, hidden, weight_rows):
    tokens, depth = hidden.shape
    out = jax.ShapeDtypeStruct((tokens, 4 * WIDTH), BF)
    return pl.pallas_call(
        prep_kernel,
        grid_spec=pltpu.PrefetchScalarGridSpec(
            num_scalar_prefetch=1,
            grid=(1,),
            in_specs=[
                pl.BlockSpec(hidden.shape, lambda i, w: (0, 0)),
                pl.BlockSpec(weight_rows.shape, lambda i, w: (0, 0)),
            ],
            out_specs=[pl.BlockSpec(out.shape, lambda i, w: (0, 0))] * 4,
            scratch_shapes=[pltpu.VMEM(weight_rows.shape, F32)],
        ),
        out_shape=[out] * 4,
        compiler_params=pltpu.CompilerParams(vmem_limit_bytes=VMEM_LIMIT),
        cost_estimate=pl.CostEstimate(
            flops=2 * tokens * depth * 16 * WIDTH * 4, bytes_accessed=4 * 2**20, transcendentals=0
        ),
        name="base_partial",
    )(where, hidden, weight_rows)


def attend_kernel(
    where, q_ref, x_ref, o_first, o_second, lse_first, lse_second, acc, top, wide, keys, values
):
    block = pl.program_id(0)
    tokens = q_ref.shape[0]
    per_tile = TILE // tokens
    tiles = 8 // per_tile

    @pl.when(block == 0)
    def _():
        acc[...] = jnp.zeros_like(acc)
        top[...] = jnp.full_like(top, LOW)
        for h in range(2):
            values[h, :, WIDTH:] = jnp.ones((KEY_BLOCK, WIDTH), BF)

    wide[...] = x_ref[...].astype(F32)
    for h in range(2):
        keys[h] = wide[pl.ds(2 * h, KEY_BLOCK, stride=4), :].astype(BF)
        values[h, :, :WIDTH] = wide[pl.ds(2 * h + 1, KEY_BLOCK, stride=4), :].astype(BF)
    for h in range(2):
        for t in range(tiles):
            first = h * 8 + t * per_tile
            q = jnp.concatenate(
                [q_ref[:, (first + j) * WIDTH : (first + j + 1) * WIDTH] for j in range(per_tile)],
                axis=0,
            )
            s = (
                lax.dot_general(q, keys[h], (((1,), (1,)), ((), ())), preferred_element_type=F32)
                * SCALE
            )
            i = h * tiles + t
            before = top[i]
            after = jnp.maximum(before, jnp.max(s, axis=1, keepdims=True))
            top[i] = after
            fade = jnp.exp2(before - after)
            p = jnp.exp2(s - after[:, :1]).astype(BF)
            acc[i] = acc[i] * jnp.concatenate([fade, fade], axis=1) + jnp.dot(
                p, values[h], preferred_element_type=F32
            )

    @pl.when(block == pl.num_programs(0) - 1)
    def _():
        half = tokens // 2
        odd = where[PARITY] == 1
        lane = lax.broadcasted_iota(jnp.int32, (tokens, WIDTH), 1)
        logs = jnp.zeros((tokens, WIDTH), F32)
        for h in range(2):
            for t in range(tiles):
                i = h * tiles + t
                total = acc[i, :, WIDTH:]
                mean = (acc[i, :, :WIDTH] / total).astype(BF)
                log = top[i] + jnp.log2(total)
                for j in range(per_tile):
                    n = h * 8 + t * per_tile + j
                    early = mean[j * tokens : j * tokens + half]
                    late = mean[j * tokens + half : (j + 1) * tokens]
                    cols = slice(n * WIDTH, (n + 1) * WIDTH)
                    o_first[:, cols] = jnp.where(odd, late, early)
                    o_second[:, cols] = jnp.where(odd, early, late)
                    logs = jnp.where(lane == n, log[j * tokens : (j + 1) * tokens], logs)
        lse_first[...] = jnp.where(odd, logs[half:], logs[:half])
        lse_second[...] = jnp.where(odd, logs[:half], logs[half:])


def attend(where, queries, cache_rows, other):
    tokens, width = NEW_TOK, queries.shape[1]
    half = tokens // 2
    blocks = cache_rows.shape[0] // 2 // 4 // KEY_BLOCK
    tiles = 16 * tokens // TILE

    def request(w):
        return 1 - w[HALF] if other else w[HALF]

    o = jax.ShapeDtypeStruct((half, width), BF)
    lse = jax.ShapeDtypeStruct((half, WIDTH), F32)
    scores = 16 * tokens * blocks * KEY_BLOCK
    return pl.pallas_call(
        attend_kernel,
        grid_spec=pltpu.PrefetchScalarGridSpec(
            num_scalar_prefetch=1,
            grid=(blocks,),
            in_specs=[
                pl.BlockSpec((tokens, width), lambda i, w: (request(w), 0)),
                pl.BlockSpec((KEY_BLOCK * 4, WIDTH), lambda i, w: (request(w) * blocks + i, 0)),
            ],
            out_specs=[pl.BlockSpec(o.shape, lambda i, w: (0, 0))] * 2
            + [pl.BlockSpec(lse.shape, lambda i, w: (0, 0))] * 2,
            scratch_shapes=[
                pltpu.VMEM((tiles, TILE, 2 * WIDTH), F32),
                pltpu.VMEM((tiles, TILE, WIDTH), F32),
                pltpu.VMEM((KEY_BLOCK * 4, WIDTH), F32),
                pltpu.VMEM((2, KEY_BLOCK, WIDTH), BF),
                pltpu.VMEM((2, KEY_BLOCK, 2 * WIDTH), BF),
            ],
        ),
        out_shape=[o, o, lse, lse],
        compiler_params=pltpu.CompilerParams(vmem_limit_bytes=VMEM_LIMIT),
        cost_estimate=pl.CostEstimate(
            flops=scores * WIDTH * 8, bytes_accessed=5 * 2**20, transcendentals=scores
        ),
        name="attend_other" if other else "attend_own",
    )(where, queries, cache_rows)


def rank_kernel(where, hidden_ref, mate_ref, own_maps, mate_maps, own_out, mate_out):
    r = pl.program_id(0)
    depth = hidden_ref.shape[1]
    for rows, maps, out, flag in (
        (hidden_ref, own_maps, own_out, HAS_OWN),
        (mate_ref, mate_maps, mate_out, HAS_MATE),
    ):
        here = where[flag + r] == 1
        part = jnp.dot(rows[...], maps[0, :depth], preferred_element_type=F32).astype(BF)
        out[0, :NEW_TOK] = jnp.where(here, part, jnp.zeros_like(part))
        up = maps[0, depth:]
        out[0, NEW_TOK:] = jnp.where(here, up, jnp.zeros_like(up))


def rank_parts(where, hidden, hidden_mate, maps):
    tokens, depth = hidden.shape
    height = maps.shape[1]
    out = jax.ShapeDtypeStruct((2, NEW_TOK + height - depth, WIDTH), BF)
    out_spec = pl.BlockSpec((1,) + out.shape[1:], lambda r, w: (r, 0, 0))
    return pl.pallas_call(
        rank_kernel,
        grid_spec=pltpu.PrefetchScalarGridSpec(
            num_scalar_prefetch=1,
            grid=(2,),
            in_specs=[
                pl.BlockSpec((NEW_TOK, depth), lambda r, w: (r, 0)),
                pl.BlockSpec((NEW_TOK, depth), lambda r, w: (r, 0)),
                pl.BlockSpec((1, height, WIDTH), lambda r, w: (w[ROW_OWN + r], 0, 0)),
                pl.BlockSpec((1, height, WIDTH), lambda r, w: (w[ROW_MATE + r], 0, 0)),
            ],
            out_specs=[out_spec, out_spec],
        ),
        out_shape=[out, out],
        name="rank_partial",
    )(where, hidden, hidden_mate, maps, maps)


def pair_kernel(where, own_ref, got_ref, mine, others):
    half = where[HALF]
    mine[...] = own_ref[half] + got_ref[half]
    others[...] = own_ref[1 - half] + got_ref[1 - half]


def pair_sum(where, own, got):
    out = jax.ShapeDtypeStruct(own.shape[1:], BF)
    whole = pl.BlockSpec(memory_space=pltpu.VMEM)
    return pl.pallas_call(
        pair_kernel,
        in_specs=[pl.BlockSpec(memory_space=pltpu.SMEM), whole, whole],
        out_specs=[whole, whole],
        out_shape=[out, out],
        name="core_sum",
    )(where, own, got)


def seq_kernel(where, own, one, two, three, rank_out, up_out):
    rank = own[:NEW_TOK].astype(F32)
    for got in (one, two, three):
        rank += got[:NEW_TOK].astype(F32)
    rank_out[...] = rank.astype(BF)
    for step, got in enumerate((own, one, two, three)):
        up_out[jnp.bitwise_xor(where[SEQ], step)] = got[NEW_TOK:]


def seq_sum(where, own, got):
    whole = pl.BlockSpec(memory_space=pltpu.VMEM)
    return pl.pallas_call(
        seq_kernel,
        in_specs=[pl.BlockSpec(memory_space=pltpu.SMEM)] + [whole] * 4,
        out_specs=[whole, whole],
        out_shape=[
            jax.ShapeDtypeStruct((NEW_TOK, WIDTH), BF),
            jax.ShapeDtypeStruct((4, own.shape[0] - NEW_TOK, WIDTH), BF),
        ],
        name="seq_sum",
    )(where, own, *got)


def final_kernel(where, q_ref, cos_ref, sin_ref, up_ref, *rest):
    ranks, bases, means, logs = rest[:4], rest[4:8], rest[8:12], rest[12:16]
    kv_out, attention_out, wide = rest[16:]
    half = q_ref.shape[0]
    start = pl.multiple_of(where[PARITY] * half, half)
    rank = sum(r[...].astype(F32) for r in ranks).astype(BF)
    base = sum(b[...].astype(F32) for b in bases)
    keys, values = [], []
    for h in range(2):
        for e in range(2):
            delta = jnp.dot(
                rank[:, e * 64 : (e + 1) * 64], up_ref[2 * e + h], preferred_element_type=F32
            )
            part = 2 * h + e
            field = base[:, part * WIDTH : (part + 1) * WIDTH] + delta
            if e == 0:
                field = field * cos_ref[...] + pltpu.roll(field, WIDTH // 2, 1) * sin_ref[...]
            wide[pl.ds(part, NEW_TOK, stride=4), :] = field
            (keys, values)[e].append(field.astype(BF))
    kv_out[...] = wide[pl.ds(start * 4, half * 4), :].astype(BF)
    row = lax.broadcasted_iota(jnp.int32, (half, NEW_TOK), 0) + start
    seen = lax.broadcasted_iota(jnp.int32, (half, NEW_TOK), 1) <= row
    old_logs = [l[...] for l in logs]
    for h in range(2):
        for j in range(8):
            n = h * 8 + j
            cols = slice(n * WIDTH, (n + 1) * WIDTH)
            s = (
                lax.dot_general(
                    q_ref[:, cols], keys[h], (((1,), (1,)), ((), ())), preferred_element_type=F32
                )
                * SCALE
            )
            s = jnp.where(seen, s, LOW)
            top = jnp.max(s, axis=1, keepdims=True)
            log = [l[:, n : n + 1] for l in old_logs]
            for l in log:
                top = jnp.maximum(top, l)
            p = jnp.exp2(s - top)
            total = jnp.sum(p, axis=1, keepdims=True)
            value = jnp.dot(p.astype(BF), values[h], preferred_element_type=F32)
            for l, mean in zip(log, means):
                weight = jnp.exp2(l - top)
                total += weight
                value += weight * mean[:, cols].astype(F32)
            attention_out[:, cols] = (value / total).astype(BF)


def final(where, queries, cos, sin, up, ranks, bases, means, logs):
    half, width = means[0].shape

    def whole(a):
        return pl.BlockSpec(a.shape, lambda i, w: (0,) * a.ndim)

    rest = [cos, sin, up, *ranks, *bases, *means, *logs]
    return pl.pallas_call(
        final_kernel,
        grid_spec=pltpu.PrefetchScalarGridSpec(
            num_scalar_prefetch=1,
            grid=(1,),
            in_specs=[pl.BlockSpec((half, width), lambda i, w: (w[SEQ], 0))]
            + [whole(a) for a in rest],
            out_specs=[
                pl.BlockSpec((half * 4, WIDTH), lambda i, w: (0, 0)),
                pl.BlockSpec((half, width), lambda i, w: (0, 0)),
            ],
            scratch_shapes=[pltpu.VMEM((NEW_TOK * 4, WIDTH), F32)],
        ),
        out_shape=[
            jax.ShapeDtypeStruct((half * 4, WIDTH), BF),
            jax.ShapeDtypeStruct((half, width), BF),
        ],
        compiler_params=pltpu.CompilerParams(vmem_limit_bytes=VMEM_LIMIT),
        name="new_kv_and_merge",
    )(where, queries, *rest)


def rotary_tables():
    exponents = jnp.arange(WIDTH // 2, dtype=F32)
    frequency = jnp.exp(exponents * (-2.0 * math.log(500000.0) / WIDTH))
    positions = CACHE + jnp.arange(NEW_TOK, dtype=jnp.int32)
    angles = positions.astype(F32)[:, None] * frequency[None, :]
    cos, sin = jnp.cos(angles), jnp.sin(angles)
    return jnp.concatenate([cos, cos], axis=1), jnp.concatenate([-sin, sin], axis=1)


def flip(axis, mask):
    return lambda a: lax.ppermute(
        a, axis, [(i, i ^ mask) for i in range(lax.axis_size(axis))]
    )


def shift(axis, step):
    size = lax.axis_size(axis)
    return lambda a: lax.ppermute(a, axis, [(i, (i + step) % size) for i in range(size)])


def local(
    hidden,
    key_value_weight,
    adapter_down_weight,
    adapter_up_weight,
    queries,
    key_value_cache,
    request_adapter,
):
    seq, group, tensor = (lax.axis_index(a) for a in ("seq", "group", "tensor"))
    core = group % 2
    own_adapter = lax.dynamic_slice_in_dim(request_adapter, 2 * group, 2)
    mate_adapter = lax.dynamic_slice_in_dim(request_adapter, 2 * (group ^ 1), 2)

    def row(adapter):
        return adapter // 8 * 4 + adapter % 4

    def here(adapter):
        return (adapter // 4 % 2 == core).astype(jnp.int32)

    where = jnp.concatenate(
        [
            jnp.stack([seq, seq // 2, seq % 2, tensor]).astype(jnp.int32),
            row(own_adapter),
            here(own_adapter),
            row(mate_adapter),
            here(mate_adapter),
        ]
    )

    quarter = lax.dynamic_slice(
        adapter_up_weight, (0, seq // 2, 0, seq % 2 * WIDTH), (4, 1, 64, WIDTH)
    )
    maps = jnp.concatenate([adapter_down_weight, quarter[:, 0]], axis=1)
    same_core = [list(range(c, lax.axis_size("group"), 2)) for c in range(2)]
    maps = lax.all_gather(maps, "group", axis_index_groups=same_core, axis=0, tiled=True)
    hidden_mate = flip("group", 1)(hidden)

    parts = prep(where, hidden, key_value_weight.reshape(-1, WIDTH))
    base = parts[0].astype(F32)
    for step in (1, 2, 3):
        base += shift("tensor", step)(parts[step]).astype(F32)
    base = base.astype(BF)
    base_own = lax.dynamic_slice_in_dim(base, seq // 2 * NEW_TOK, NEW_TOK, 0)
    base_other = lax.dynamic_slice_in_dim(base, (1 - seq // 2) * NEW_TOK, NEW_TOK, 0)
    bases = [
        base_own,
        flip("seq", 1)(base_own),
        flip("seq", 2)(base_other),
        flip("seq", 3)(base_other),
    ]

    cache_rows = key_value_cache.reshape(-1, WIDTH)
    o2, o3, l2, l3 = attend(where, queries, cache_rows, True)
    o0, o1, l0, l1 = attend(where, queries, cache_rows, False)
    means = [o0, flip("seq", 1)(o1), flip("seq", 2)(o2), flip("seq", 3)(o3)]
    logs = [l0, flip("seq", 1)(l1), flip("seq", 2)(l2), flip("seq", 3)(l3)]

    own, mate = rank_parts(where, hidden, hidden_mate, maps)
    mine, others = pair_sum(where, own, flip("group", 1)(mate))
    rank, up = seq_sum(
        where, mine, [flip("seq", 1)(mine), flip("seq", 2)(others), flip("seq", 3)(others)]
    )
    ranks = [rank] + [shift("tensor", step)(rank) for step in (1, 2, 3)]

    cos, sin = rotary_tables()
    new_kv, attention = final(where, queries, cos, sin, up, ranks, bases, means, logs)
    return new_kv.reshape(-1, 2, 2, WIDTH), attention


def solution(mesh):
    in_specs = (
        P("group", ("tensor", "seq")),
        P(("tensor", "seq"), None, None, None),
        P("group", ("tensor", "seq"), None),
        P("group", None, None, "tensor"),
        P("group", "tensor"),
        P("group", "seq", "tensor", None, None),
        P(),
    )
    out_specs = (P(("group", "seq"), "tensor", None, None), P(("group", "seq"), "tensor"))
    return jax.shard_map(local, mesh=mesh, in_specs=in_specs, out_specs=out_specs, check_vma=False)
```

time: 378 us -> 130 us (0.34)
  the two profiles are of different devices: /device:TPU:32 before, /device:TPU:8 now
where the time goes in v1:
time: 130 us; the launch traced here: 129 us
  Pallas kernels  54.7 us (42%)
  starting transfers between devices  29.7 us (23%)
  waiting for transfers between devices  23.7 us (18%)
  between operations  14.4 us (11%)
  other arithmetic  4.78 us (4%)
  local copies, waits for them, and re-layouts  2.17 us (2%)
    pallas_call x2, Pallas kernels, attend(): pl.pallas_call(attend_kernel, grid_spec=pltpu.PrefetchScalarGridSpec(num_...  34.8 us
    ppermute x14, starting transfers between devices, flip(): lax.ppermute(a, axis, [(i, i ^ mask) for i in range(lax.axis_size(axis))])  19.3 us
    all_gather x1, waiting for transfers between devices, local(): lax.all_gather(maps, 'group', axis_index_groups=same_core, axis=0, tiled=...  13.6 us
    ppermute x6, starting transfers between devices, shift(): lax.ppermute(a, axis, [(i, (i + step) % size) for i in range(size)])  10.4 us
    pallas_call x1, Pallas kernels, final(): pl.pallas_call(final_kernel, grid_spec=pltpu.PrefetchScalarGridSpec(num_s...  8.87 us
    ppermute x14, waiting for transfers between devices, flip(): lax.ppermute(a, axis, [(i, i ^ mask) for i in range(lax.axis_size(axis))])  8.18 us
    pallas_call x1, Pallas kernels, prep(): pl.pallas_call(prep_kernel, grid_spec=pltpu.PrefetchScalarGridSpec(num_sc...  4.98 us
    pallas_call x1, Pallas kernels, rank_parts(): pl.pallas_call(rank_kernel, grid_spec=pltpu.PrefetchScalarGridSpec(num_sc...  2.89 us
  transfers between devices with their start and end apart: 21, of which 6 were waited for; matrix products, arithmetic and copies ran while one was open for 3% of the time, Pallas kernels for 35%

profile of v1, /device:TPU:8, one launch (start us, length us, event | category | flops | bytes accessed | tf_op | source)
XLA Modules:
  0.0 129.4 jit_solution(5400093541981616434)
XLA Ops:
  7.2 0.0 copy-start
  7.2 0.0 all-gather.2.cloned.1.call-start
  7.3 0.9 copy-done
  8.1 1.9 %pad_maximum_fusion = bf16[4,576,128]{2,1,0:T(8,128)(2,1)} fusion(bf16[4,64,128]{2,1,0:T(8,128)(2,1)S(1)} %dynamic-slice_bitcast_fusion, bf16[4,512,128]{2,1,0:T(8,128)(2,1)} %param.9), kind=kLoop, calls=%fused_computation | loop fusion | flops 1179648 | bytes 1179648 | tf_op jit(solution)/shard_map/concatenate | solution.py:376
  10.1 0.0 all-gather.2.cloned.1.call-update
  10.1 0.1 collective-permute-start
  10.2 0.8 fusion.2
  11.0 0.8 compare_convert_fusion
  11.9 0.7 concatenate.12.where
  12.5 5.0 %base_partial.1 = (bf16[256,512]{1,0:T(8,128)(2,1)}, bf16[256,512]{1,0:T(8,128)(2,1)}, bf16[256,512]{1,0:T(8,128)(2,1)}, bf16[256,512]{1,0:T(8,128)(2,1)}) custom-call(s32[12]{0:T(128)} %concatenate.12.where, bf16[256,512]{1,0:T(8,128)(2,1)} %hidden_ref.3, bf16[8192,128]{1,0:T(8,128)(2,1)} %bitcast.11), custom_call_target="tpu_custom_call" | custom-call | flops 2147483648 | bytes 4194304 | tf_op jit(solution)/shard_map/base_partial/pallas_call | solution.py:43
  17.5 2.8 %collective-permute-start.10 = (bf16[256,512]{1,0:T(8,128)(2,1)}, bf16[256,512]{1,0:T(8,128)(2,1)S(1)}, u32[]{:S(2)}, u32[]{:S(2)}) collective-permute-start(bf16[256,512]{1,0:T(8,128)(2,1)} %get-tuple-element.31), channel_id=1, source_target_pairs={{0,12},{4,0},{8,4},{12,8},{1,13},{5,1},{9,5},{13,9},{2,14},{6,2},{... | collective-permute-start | bytes 786440 | tf_op jit(solution)/shard_map/ppermute | solution.py:340
  20.3 0.8 collective-permute-start.9
  21.1 0.9 collective-permute-start.8
  22.0 17.4 %attend_own.1 = (bf16[64,2048]{1,0:T(8,128)(2,1)}, bf16[64,2048]{1,0:T(8,128)(2,1)}, f32[64,128]{1,0:T(8,128)}, f32[64,128]{1,0:T(8,128)}) custom-call(s32[12]{0:T(128)} %concatenate.12.where, bf16[256,2048]{1,0:T(8,128)(2,1)} %q_ref.5, bf16[32768,128]{1,0:T(8,128)(2,1)} %bitcast.9), custom_call_target="tpu_custom_call" | custom-call | flops 8589934592 | bytes 5242880 | tf_op jit(solution)/shard_map/attend_own/pallas_call | solution.py:140
  39.4 0.7 collective-permute-start.14
  40.1 17.4 %attend_other.1 = (bf16[64,2048]{1,0:T(8,128)(2,1)}, bf16[64,2048]{1,0:T(8,128)(2,1)}, f32[64,128]{1,0:T(8,128)}, f32[64,128]{1,0:T(8,128)}) custom-call(s32[12]{0:T(128)} %concatenate.12.where, bf16[256,2048]{1,0:T(8,128)(2,1)} %q_ref.5, bf16[32768,128]{1,0:T(8,128)(2,1)} %bitcast.10), custom_call_target="tpu_custom_call" | custom-call | flops 8589934592 | bytes 5242880 | tf_op jit(solution)/shard_map/attend_other/pallas_call | solution.py:140
  57.5 0.0 collective-permute-done.mate_ref
  57.5 0.0 copy-start.3
  57.6 1.7 %collective-permute-start.17 = (f32[64,128]{1,0:T(8,128)S(1)}, f32[64,128]{1,0:T(8,128)S(1)}, u32[]{:S(2)}, u32[]{:S(2)}) collective-permute-start(f32[64,128]{1,0:T(8,128)S(1)} %copy-done.23), channel_id=1, source_target_pairs={{0,1},{1,0},{2,3},{3,2},{4,5},{5,4},{6,7},{7,6},{8,9},{9,8},{10,11... | collective-permute-start | bytes 98312 | tf_op jit(solution)/shard_map/ppermute | solution.py:333
  59.3 13.6 %all-gather.2.cloned.1.call-done.own_maps.mate_maps = bf16[32,576,128]{2,1,0:T(8,128)(2,1)} async-done(((bf16[4,576,128]{2,1,0:T(8,128)(2,1)}), bf16[32,576,128]{2,1,0:T(8,128)(2,1)}) %all-gather.2.cloned.1.call-update) | async-done | bytes 4718608 | tf_op jit(solution)/shard_map/all_gather | solution.py:378
  72.9 2.9 %rank_partial.1 = (bf16[2,192,128]{2,1,0:T(8,128)(2,1)}, bf16[2,192,128]{2,1,0:T(8,128)(2,1)}) custom-call(s32[12]{0:T(128)} %concatenate.12.where, bf16[256,512]{1,0:T(8,128)(2,1)} %hidden_ref.3, bf16[256,512]{1,0:T(8,128)(2,1)} %copy-done.3, bf16[32,576,128]{2,1,0:T(8,128)(2,1)} %all-gather.2.cloned.1.call-done.own_maps.mate_maps, ...), custom_call_target="tpu_custom_call" | custom-call | tf_op jit(solution)/shard_map/rank_partial/pallas_call | solution.py:187
  75.7 0.0 collective-permute-done.10
  75.8 2.2 %collective-permute-start.18 = (f32[64,128]{1,0:T(8,128)S(1)}, f32[64,128]{1,0:T(8,128)S(1)}, u32[]{:S(2)}, u32[]{:S(2)}) collective-permute-start(f32[64,128]{1,0:T(8,128)S(1)} %copy-done.24), channel_id=1, source_target_pairs={{0,2},{1,3},{2,0},{3,1},{4,6},{5,7},{6,4},{7,5},{8,10},{9,11},{10,... | collective-permute-start | bytes 98312 | tf_op jit(solution)/shard_map/ppermute | solution.py:333
  78.0 0.0 collective-permute-done.9
  78.0 0.0 collective-permute-start.19
  78.0 0.0 collective-permute-done.8
  78.0 0.1 collective-permute-start.1
  78.1 0.1 add_convert_fusion
  78.2 1.3 %collective-permute-done.1.got_ref = bf16[2,192,128]{2,1,0:T(8,128)(2,1)S(1)} collective-permute-done((bf16[2,192,128]{2,1,0:T(8,128)(2,1)}, bf16[2,192,128]{2,1,0:T(8,128)(2,1)S(1)}, u32[]{:S(2)}, u32[]{:S(2)}) %collective-permute-start.1) | collective-permute-done | bytes 98336 | tf_op jit(solution)/shard_map/ppermute | solution.py:333
  79.6 3.4 %collective-permute-start.15 = (bf16[64,2048]{1,0:T(8,128)(2,1)S(1)}, bf16[64,2048]{1,0:T(8,128)(2,1)S(1)}, u32[]{:S(2)}, u32[]{:S(2)}) collective-permute-start(bf16[64,2048]{1,0:T(8,128)(2,1)S(1)} %copy-done.21), channel_id=1, source_target_pairs={{0,2},{1,3},{2,0},{3,1},{4,6},{5,7},{6,4},{7,5},{8,10},{9,11},{10,... | collective-permute-start | bytes 786440 | tf_op jit(solution)/shard_map/ppermute | solution.py:333
  83.0 0.0 copy-done.10
  83.0 1.6 %core_sum.1 = (bf16[192,128]{1,0:T(8,128)(2,1)}, bf16[192,128]{1,0:T(8,128)(2,1)}) custom-call(s32[12]{0:T(128)} %concatenate.12.where, bf16[2,192,128]{2,1,0:T(8,128)(2,1)} %get-tuple-element.22.own_ref, bf16[2,192,128]{2,1,0:T(8,128)(2,1)} %copy-done.10), custom_call_target="tpu_custom_call" | custom-call | tf_op jit(solution)/shard_map/core_sum/pallas_call | solution.py:214
  84.6 0.0 collective-permute-done.17.rest_13_
  84.6 0.6 collective-permute-start.16
  85.2 0.0 collective-permute-done.18.rest_14_
  85.2 2.1 %collective-permute-start.3 = (bf16[192,128]{1,0:T(8,128)(2,1)}, bf16[192,128]{1,0:T(8,128)(2,1)S(1)}, u32[]{:S(2)}, u32[]{:S(2)}) collective-permute-start(bf16[192,128]{1,0:T(8,128)(2,1)} %get-tuple-element.25), channel_id=1, source_target_pairs={{0,2},{1,3},{2,0},{3,1},{4,6},{5,7},{6,4},{7,5},{8,10},{9,11},{10,... | collective-permute-start | bytes 147464 | tf_op jit(solution)/shard_map/ppermute | solution.py:333
  87.4 0.0 collective-permute-done.19.rest_15_
  87.4 0.6 collective-permute-start.4
  88.0 0.0 collective-permute-done.14.rest_9_
  88.0 2.0 %collective-permute-start.2 = (bf16[192,128]{1,0:T(8,128)(2,1)}, bf16[192,128]{1,0:T(8,128)(2,1)S(1)}, u32[]{:S(2)}, u32[]{:S(2)}) collective-permute-start(bf16[192,128]{1,0:T(8,128)(2,1)} %get-tuple-element.24.own), channel_id=1, source_target_pairs={{0,1},{1,0},{2,3},{3,2},{4,5},{5,4},{6,7},{7,6},{8,9},{9,8},{10,11... | collective-permute-start | bytes 147464 | tf_op jit(solution)/shard_map/ppermute | solution.py:333
  90.0 0.0 copy-start.1
  90.0 2.3 %collective-permute-done.2.one = bf16[192,128]{1,0:T(8,128)(2,1)S(1)} collective-permute-done((bf16[192,128]{1,0:T(8,128)(2,1)}, bf16[192,128]{1,0:T(8,128)(2,1)S(1)}, u32[]{:S(2)}, u32[]{:S(2)}) %collective-permute-start.2) | collective-permute-done | bytes 49184 | tf_op jit(solution)/shard_map/ppermute | solution.py:333
  92.3 2.9 %collective-permute-start.12 = (bf16[128,512]{1,0:T(8,128)(2,1)S(1)}, bf16[128,512]{1,0:T(8,128)(2,1)S(1)}, u32[]{:S(2)}, u32[]{:S(2)}) collective-permute-start(bf16[128,512]{1,0:T(8,128)(2,1)S(1)} %get-tuple-element.42), channel_id=1, source_target_pairs={{0,2},{1,3},{2,0},{3,1},{4,6},{5,7},{6,4},{7,5},{8,10},{9,11},{10,... | collective-permute-start | bytes 393224 | tf_op jit(solution)/shard_map/ppermute | solution.py:333
  95.2 0.0 collective-permute-done.3.two
  95.2 0.5 collective-permute-start.13
  95.7 4.5 %collective-permute-done.4.three = bf16[192,128]{1,0:T(8,128)(2,1)S(1)} collective-permute-done((bf16[192,128]{1,0:T(8,128)(2,1)}, bf16[192,128]{1,0:T(8,128)(2,1)S(1)}, u32[]{:S(2)}, u32[]{:S(2)}) %collective-permute-start.4) | collective-permute-done | bytes 49184 | tf_op jit(solution)/shard_map/ppermute | solution.py:333
  100.2 2.3 %collective-permute-start.11 = (bf16[128,512]{1,0:T(8,128)(2,1)S(1)}, bf16[128,512]{1,0:T(8,128)(2,1)S(1)}, u32[]{:S(2)}, u32[]{:S(2)}) collective-permute-start(bf16[128,512]{1,0:T(8,128)(2,1)S(1)} %get-tuple-element.43.rest_4_), channel_id=1, source_target_pairs={{0,1},{1,0},{2,3},{3,2},{4,5},{5,4},{6,7},{7,6},{8,9},{9,8},{10,11... | collective-permute-start | bytes 393224 | tf_op jit(solution)/shard_map/ppermute | solution.py:333
  102.6 0.3 fusion
  102.9 1.5 %seq_sum.1 = (bf16[128,128]{1,0:T(8,128)(2,1)}, bf16[4,64,128]{2,1,0:T(8,128)(2,1)}) custom-call(s32[12]{0:T(128)} %concatenate.12.where, bf16[192,128]{1,0:T(8,128)(2,1)} %get-tuple-element.24.own, bf16[192,128]{1,0:T(8,128)(2,1)} %copy-done.13, bf16[192,128]{1,0:T(8,128)(2,1)} %copy-done.11, bf16[192,128]{1,0:T(8,128)(2,1)} %copy-done.12), custom_call_target="tpu_custom_call" | custom-call | tf_op jit(solution)/shard_map/seq_sum/pallas_call | solution.py:234
  104.4 0.0 collective-permute-done.15.rest_10_
  104.4 1.8 %collective-permute-start.5 = (bf16[128,128]{1,0:T(8,128)(2,1)}, bf16[128,128]{1,0:T(8,128)(2,1)S(1)}, u32[]{:S(2)}, u32[]{:S(2)}) collective-permute-start(bf16[128,128]{1,0:T(8,128)(2,1)} %get-tuple-element.27.rest_0_), channel_id=1, source_target_pairs={{0,4},{4,8},{8,12},{12,0},{1,5},{5,9},{9,13},{13,1},{2,6},{6,10},{... | collective-permute-start | bytes 98312 | tf_op jit(solution)/shard_map/ppermute | solution.py:340
  106.2 0.0 collective-permute-done.16.rest_11_
  106.2 2.7 %collective-permute-start.6 = (bf16[128,128]{1,0:T(8,128)(2,1)}, bf16[128,128]{1,0:T(8,128)(2,1)S(1)}, u32[]{:S(2)}, u32[]{:S(2)}) collective-permute-start(bf16[128,128]{1,0:T(8,128)(2,1)} %get-tuple-element.27.rest_0_), channel_id=1, source_target_pairs={{0,8},{4,12},{8,0},{12,4},{1,9},{5,13},{9,1},{13,5},{2,10},{6,14},... | collective-permute-start | bytes 98312 | tf_op jit(solution)/shard_map/ppermute | solution.py:340
  108.9 0.0 collective-permute-done.11.rest_5_
  108.9 1.5 %collective-permute-start.7 = (bf16[128,128]{1,0:T(8,128)(2,1)}, bf16[128,128]{1,0:T(8,128)(2,1)S(1)}, u32[]{:S(2)}, u32[]{:S(2)}) collective-permute-start(bf16[128,128]{1,0:T(8,128)(2,1)} %get-tuple-element.27.rest_0_), channel_id=1, source_target_pairs={{0,12},{4,0},{8,4},{12,8},{1,13},{5,1},{9,5},{13,9},{2,14},{6,2},{... | collective-permute-start | bytes 98312 | tf_op jit(solution)/shard_map/ppermute | solution.py:340
  110.4 0.7 pad_maximum_fusion.1
  111.1 0.0 collective-permute-done.12.rest_6_
  111.1 0.0 collective-permute-done.13.rest_7_
  111.1 0.0 collective-permute-done.5.rest_1_
  111.2 0.0 copy-start.17
  111.2 0.7 collective-permute-done.6.rest_2_
  111.9 1.2 collective-permute-done.7.rest_3_
  113.1 0.5 copy-done.19
  113.7 8.9 %new_kv_and_merge.1 = (bf16[256,128]{1,0:T(8,128)(2,1)}, bf16[64,2048]{1,0:T(8,128)(2,1)}) custom-call(s32[12]{0:T(128)} %concatenate.12.where, bf16[256,2048]{1,0:T(8,128)(2,1)} %q_ref.5, f32[128,128]{1,0:T(8,128)} %get-tuple-element.51.cos_ref, f32[128,128]{1,0:T(8,128)} %get-tuple-element.52.sin_ref, bf16[4,64,128]{2,1,0:T(8,128)(2,1)} %get-tuple-element.26.up_ref, ...), custom_call_target="tpu_custom_call" | custom-call | tf_op jit(solution)/shard_map/new_kv_and_merge/pallas_call | solution.py:301
  (47 shorter events, 0.1 us)
Async XLA Ops:
  7.2 1.0 copy-start
  7.2 65.7 %all-gather.2.cloned.1.call-start = ((), (), s32[]{:S(2)}) async-start(), calls=%async_computation | async-start | bytes 5308416 | tf_op jit(solution)/shard_map/all_gather | solution.py:378
  10.1 47.4 %collective-permute-start = (bf16[256,512]{1,0:T(8,128)(2,1)}, bf16[256,512]{1,0:T(8,128)(2,1)S(1)}, u32[]{:S(2)}, u32[]{:S(2)}) collective-permute-start(bf16[256,512]{1,0:T(8,128)(2,1)} %hidden_ref.3), channel_id=1, source_target_pairs={{0,16},{16,0},{32,48},{48,32},{64,80},{80,64},{96,112},{112,96},{1... | collective-permute-start | bytes 786440 | tf_op jit(solution)/shard_map/ppermute | solution.py:333
  17.5 58.3 %collective-permute-start.10 = (bf16[256,512]{1,0:T(8,128)(2,1)}, bf16[256,512]{1,0:T(8,128)(2,1)S(1)}, u32[]{:S(2)}, u32[]{:S(2)}) collective-permute-start(bf16[256,512]{1,0:T(8,128)(2,1)} %get-tuple-element.31), channel_id=1, source_target_pairs={{0,12},{4,0},{8,4},{12,8},{1,13},{5,1},{9,5},{13,9},{2,14},{6,2},{... | collective-permute-start | bytes 786440 | tf_op jit(solution)/shard_map/ppermute | solution.py:340
  20.3 57.7 %collective-permute-start.9 = (bf16[256,512]{1,0:T(8,128)(2,1)}, bf16[256,512]{1,0:T(8,128)(2,1)S(1)}, u32[]{:S(2)}, u32[]{:S(2)}) collective-permute-start(bf16[256,512]{1,0:T(8,128)(2,1)} %get-tuple-element.30), channel_id=1, source_target_pairs={{0,8},{4,12},{8,0},{12,4},{1,9},{5,13},{9,1},{13,5},{2,10},{6,14},... | collective-permute-start | bytes 786440 | tf_op jit(solution)/shard_map/ppermute | solution.py:340
  21.1 56.9 %collective-permute-start.8 = (bf16[256,512]{1,0:T(8,128)(2,1)}, bf16[256,512]{1,0:T(8,128)(2,1)S(1)}, u32[]{:S(2)}, u32[]{:S(2)}) collective-permute-start(bf16[256,512]{1,0:T(8,128)(2,1)} %get-tuple-element.29), channel_id=1, source_target_pairs={{0,4},{4,8},{8,12},{12,0},{1,5},{5,9},{9,13},{13,1},{2,6},{6,10},{... | collective-permute-start | bytes 786440 | tf_op jit(solution)/shard_map/ppermute | solution.py:340
  39.4 18.2 %copy-start.23 = (f32[64,128]{1,0:T(8,128)S(1)}, f32[64,128]{1,0:T(8,128)}, u32[]{:S(2)}) copy-start(f32[64,128]{1,0:T(8,128)} %get-tuple-element.37) | copy-start | bytes 98308
  39.4 48.6 %collective-permute-start.14 = (bf16[64,2048]{1,0:T(8,128)(2,1)}, bf16[64,2048]{1,0:T(8,128)(2,1)S(1)}, u32[]{:S(2)}, u32[]{:S(2)}) collective-permute-start(bf16[64,2048]{1,0:T(8,128)(2,1)} %get-tuple-element.33), channel_id=1, source_target_pairs={{0,1},{1,0},{2,3},{3,2},{4,5},{5,4},{6,7},{7,6},{8,9},{9,8},{10,11... | collective-permute-start | bytes 786440 | tf_op jit(solution)/shard_map/ppermute | solution.py:333
  57.5 15.3 %copy-start.3 = (bf16[256,512]{1,0:T(8,128)(2,1)}, bf16[256,512]{1,0:T(8,128)(2,1)S(1)}, u32[]{:S(2)}) copy-start(bf16[256,512]{1,0:T(8,128)(2,1)S(1)} %collective-permute-done.mate_ref) | copy-start | bytes 786436
  57.6 18.2 %copy-start.24 = (f32[64,128]{1,0:T(8,128)S(1)}, f32[64,128]{1,0:T(8,128)}, u32[]{:S(2)}) copy-start(f32[64,128]{1,0:T(8,128)} %get-tuple-element.38) | copy-start | bytes 98308
  57.6 20.4 %copy-start.22 = (f32[64,128]{1,0:T(8,128)S(1)}, f32[64,128]{1,0:T(8,128)}, u32[]{:S(2)}) copy-start(f32[64,128]{1,0:T(8,128)} %get-tuple-element.39) | copy-start | bytes 98308
  57.6 20.5 %copy-start.6 = (bf16[256,512]{1,0:T(8,128)(2,1)S(1)}, bf16[256,512]{1,0:T(8,128)(2,1)}, u32[]{:S(2)}) copy-start(bf16[256,512]{1,0:T(8,128)(2,1)} %get-tuple-element.28) | copy-start | bytes 786436
  57.6 22.0 %copy-start.21 = (bf16[64,2048]{1,0:T(8,128)(2,1)S(1)}, bf16[64,2048]{1,0:T(8,128)(2,1)}, u32[]{:S(2)}) copy-start(bf16[64,2048]{1,0:T(8,128)(2,1)} %get-tuple-element.34) | copy-start | bytes 786436
  57.6 27.0 %copy-start.20 = (bf16[64,2048]{1,0:T(8,128)(2,1)S(1)}, bf16[64,2048]{1,0:T(8,128)(2,1)}, u32[]{:S(2)}) copy-start(bf16[64,2048]{1,0:T(8,128)(2,1)} %get-tuple-element.35) | copy-start | bytes 786436
  57.6 27.0 %collective-permute-start.17 = (f32[64,128]{1,0:T(8,128)S(1)}, f32[64,128]{1,0:T(8,128)S(1)}, u32[]{:S(2)}, u32[]{:S(2)}) collective-permute-start(f32[64,128]{1,0:T(8,128)S(1)} %copy-done.23), channel_id=1, source_target_pairs={{0,1},{1,0},{2,3},{3,2},{4,5},{5,4},{6,7},{7,6},{8,9},{9,8},{10,11... | collective-permute-start | bytes 98312 | tf_op jit(solution)/shard_map/ppermute | solution.py:333
  75.8 9.5 %collective-permute-start.18 = (f32[64,128]{1,0:T(8,128)S(1)}, f32[64,128]{1,0:T(8,128)S(1)}, u32[]{:S(2)}, u32[]{:S(2)}) collective-permute-start(f32[64,128]{1,0:T(8,128)S(1)} %copy-done.24), channel_id=1, source_target_pairs={{0,2},{1,3},{2,0},{3,1},{4,6},{5,7},{6,4},{7,5},{8,10},{9,11},{10,... | collective-permute-start | bytes 98312 | tf_op jit(solution)/shard_map/ppermute | solution.py:333
  78.0 9.4 %collective-permute-start.19 = (f32[64,128]{1,0:T(8,128)S(1)}, f32[64,128]{1,0:T(8,128)S(1)}, u32[]{:S(2)}, u32[]{:S(2)}) collective-permute-start(f32[64,128]{1,0:T(8,128)S(1)} %copy-done.22), channel_id=1, source_target_pairs={{0,3},{1,2},{2,1},{3,0},{4,7},{5,6},{6,5},{7,4},{8,11},{9,10},{10,... | collective-permute-start | bytes 98312 | tf_op jit(solution)/shard_map/ppermute | solution.py:333
  78.0 1.6 %collective-permute-start.1 = (bf16[2,192,128]{2,1,0:T(8,128)(2,1)}, bf16[2,192,128]{2,1,0:T(8,128)(2,1)S(1)}, u32[]{:S(2)}, u32[]{:S(2)}) collective-permute-start(bf16[2,192,128]{2,1,0:T(8,128)(2,1)} %get-tuple-element.23), channel_id=1, source_target_pairs={{0,16},{16,0},{32,48},{48,32},{64,80},{80,64},{96,112},{112,96},{1... | collective-permute-start | bytes 294920 | tf_op jit(solution)/shard_map/ppermute | solution.py:333
  79.6 3.4 %copy-start.10 = (bf16[2,192,128]{2,1,0:T(8,128)(2,1)}, bf16[2,192,128]{2,1,0:T(8,128)(2,1)S(1)}, u32[]{:S(2)}) copy-start(bf16[2,192,128]{2,1,0:T(8,128)(2,1)S(1)} %collective-permute-done.1.got_ref) | copy-start | bytes 294916
  79.6 24.9 %collective-permute-start.15 = (bf16[64,2048]{1,0:T(8,128)(2,1)S(1)}, bf16[64,2048]{1,0:T(8,128)(2,1)S(1)}, u32[]{:S(2)}, u32[]{:S(2)}) collective-permute-start(bf16[64,2048]{1,0:T(8,128)(2,1)S(1)} %copy-done.21), channel_id=1, source_target_pairs={{0,2},{1,3},{2,0},{3,1},{4,6},{5,7},{6,4},{7,5},{8,10},{9,11},{10,... | collective-permute-start | bytes 786440 | tf_op jit(solution)/shard_map/ppermute | solution.py:333
  84.6 28.4 %copy-start.14 = (f32[64,128]{1,0:T(8,128)}, f32[64,128]{1,0:T(8,128)S(1)}, u32[]{:S(2)}) copy-start(f32[64,128]{1,0:T(8,128)S(1)} %collective-permute-done.17.rest_13_) | copy-start | bytes 98308
  84.6 21.6 %collective-permute-start.16 = (bf16[64,2048]{1,0:T(8,128)(2,1)S(1)}, bf16[64,2048]{1,0:T(8,128)(2,1)S(1)}, u32[]{:S(2)}, u32[]{:S(2)}) collective-permute-start(bf16[64,2048]{1,0:T(8,128)(2,1)S(1)} %copy-done.20), channel_id=1, source_target_pairs={{0,3},{1,2},{2,1},{3,0},{4,7},{5,6},{6,5},{7,4},{8,11},{9,10},{10,... | collective-permute-start | bytes 786440 | tf_op jit(solution)/shard_map/ppermute | solution.py:333
  85.2 27.8 %copy-start.15 = (f32[64,128]{1,0:T(8,128)}, f32[64,128]{1,0:T(8,128)S(1)}, u32[]{:S(2)}) copy-start(f32[64,128]{1,0:T(8,128)S(1)} %collective-permute-done.18.rest_14_) | copy-start | bytes 98308
  85.2 9.9 %collective-permute-start.3 = (bf16[192,128]{1,0:T(8,128)(2,1)}, bf16[192,128]{1,0:T(8,128)(2,1)S(1)}, u32[]{:S(2)}, u32[]{:S(2)}) collective-permute-start(bf16[192,128]{1,0:T(8,128)(2,1)} %get-tuple-element.25), channel_id=1, source_target_pairs={{0,2},{1,3},{2,0},{3,1},{4,6},{5,7},{6,4},{7,5},{8,10},{9,11},{10,... | collective-permute-start | bytes 147464 | tf_op jit(solution)/shard_map/ppermute | solution.py:333
  87.4 25.7 %copy-start.16 = (f32[64,128]{1,0:T(8,128)}, f32[64,128]{1,0:T(8,128)S(1)}, u32[]{:S(2)}) copy-start(f32[64,128]{1,0:T(8,128)S(1)} %collective-permute-done.19.rest_15_) | copy-start | bytes 98308
  87.4 12.9 %collective-permute-start.4 = (bf16[192,128]{1,0:T(8,128)(2,1)}, bf16[192,128]{1,0:T(8,128)(2,1)S(1)}, u32[]{:S(2)}, u32[]{:S(2)}) collective-permute-start(bf16[192,128]{1,0:T(8,128)(2,1)} %get-tuple-element.25), channel_id=1, source_target_pairs={{0,3},{1,2},{2,1},{3,0},{4,7},{5,6},{6,5},{7,4},{8,11},{9,10},{10,... | collective-permute-start | bytes 147464 | tf_op jit(solution)/shard_map/ppermute | solution.py:333
  88.0 25.1 %copy-start.2 = (bf16[64,2048]{1,0:T(8,128)(2,1)}, bf16[64,2048]{1,0:T(8,128)(2,1)S(1)}, u32[]{:S(2)}) copy-start(bf16[64,2048]{1,0:T(8,128)(2,1)S(1)} %collective-permute-done.14.rest_9_) | copy-start | bytes 786436
  88.0 4.3 %collective-permute-start.2 = (bf16[192,128]{1,0:T(8,128)(2,1)}, bf16[192,128]{1,0:T(8,128)(2,1)S(1)}, u32[]{:S(2)}, u32[]{:S(2)}) collective-permute-start(bf16[192,128]{1,0:T(8,128)(2,1)} %get-tuple-element.24.own), channel_id=1, source_target_pairs={{0,1},{1,0},{2,3},{3,2},{4,5},{5,4},{6,7},{7,6},{8,9},{9,8},{10,11... | collective-permute-start | bytes 147464 | tf_op jit(solution)/shard_map/ppermute | solution.py:333
  90.0 23.1 %copy-start.1 = (bf16[128,512]{1,0:T(8,128)(2,1)}, bf16[128,512]{1,0:T(8,128)(2,1)S(1)}, u32[]{:S(2)}) copy-start(bf16[128,512]{1,0:T(8,128)(2,1)S(1)} %get-tuple-element.43.rest_4_) | copy-start | bytes 393220
  92.3 10.6 %copy-start.13 = (bf16[192,128]{1,0:T(8,128)(2,1)}, bf16[192,128]{1,0:T(8,128)(2,1)S(1)}, u32[]{:S(2)}) copy-start(bf16[192,128]{1,0:T(8,128)(2,1)S(1)} %collective-permute-done.2.one) | copy-start | bytes 147460
  92.3 18.8 %collective-permute-start.12 = (bf16[128,512]{1,0:T(8,128)(2,1)S(1)}, bf16[128,512]{1,0:T(8,128)(2,1)S(1)}, u32[]{:S(2)}, u32[]{:S(2)}) collective-permute-start(bf16[128,512]{1,0:T(8,128)(2,1)S(1)} %get-tuple-element.42), channel_id=1, source_target_pairs={{0,2},{1,3},{2,0},{3,1},{4,6},{5,7},{6,4},{7,5},{8,10},{9,11},{10,... | collective-permute-start | bytes 393224 | tf_op jit(solution)/shard_map/ppermute | solution.py:333
  95.2 7.7 %copy-start.11 = (bf16[192,128]{1,0:T(8,128)(2,1)}, bf16[192,128]{1,0:T(8,128)(2,1)S(1)}, u32[]{:S(2)}) copy-start(bf16[192,128]{1,0:T(8,128)(2,1)S(1)} %collective-permute-done.3.two) | copy-start | bytes 147460
  95.2 15.9 %collective-permute-start.13 = (bf16[128,512]{1,0:T(8,128)(2,1)S(1)}, bf16[128,512]{1,0:T(8,128)(2,1)S(1)}, u32[]{:S(2)}, u32[]{:S(2)}) collective-permute-start(bf16[128,512]{1,0:T(8,128)(2,1)S(1)} %get-tuple-element.42), channel_id=1, source_target_pairs={{0,3},{1,2},{2,1},{3,0},{4,7},{5,6},{6,5},{7,4},{8,11},{9,10},{10,... | collective-permute-start | bytes 393224 | tf_op jit(solution)/shard_map/ppermute | solution.py:333
  100.2 2.7 %copy-start.12 = (bf16[192,128]{1,0:T(8,128)(2,1)}, bf16[192,128]{1,0:T(8,128)(2,1)S(1)}, u32[]{:S(2)}) copy-start(bf16[192,128]{1,0:T(8,128)(2,1)S(1)} %collective-permute-done.4.three) | copy-start | bytes 147460
  100.2 8.7 %collective-permute-start.11 = (bf16[128,512]{1,0:T(8,128)(2,1)S(1)}, bf16[128,512]{1,0:T(8,128)(2,1)S(1)}, u32[]{:S(2)}, u32[]{:S(2)}) collective-permute-start(bf16[128,512]{1,0:T(8,128)(2,1)S(1)} %get-tuple-element.43.rest_4_), channel_id=1, source_target_pairs={{0,1},{1,0},{2,3},{3,2},{4,5},{5,4},{6,7},{7,6},{8,9},{9,8},{10,11... | collective-permute-start | bytes 393224 | tf_op jit(solution)/shard_map/ppermute | solution.py:333
  104.4 8.6 %copy-start.4 = (bf16[64,2048]{1,0:T(8,128)(2,1)}, bf16[64,2048]{1,0:T(8,128)(2,1)S(1)}, u32[]{:S(2)}) copy-start(bf16[64,2048]{1,0:T(8,128)(2,1)S(1)} %collective-permute-done.15.rest_10_) | copy-start | bytes 786436
  104.4 6.7 %collective-permute-start.5 = (bf16[128,128]{1,0:T(8,128)(2,1)}, bf16[128,128]{1,0:T(8,128)(2,1)S(1)}, u32[]{:S(2)}, u32[]{:S(2)}) collective-permute-start(bf16[128,128]{1,0:T(8,128)(2,1)} %get-tuple-element.27.rest_0_), channel_id=1, source_target_pairs={{0,4},{4,8},{8,12},{12,0},{1,5},{5,9},{9,13},{13,1},{2,6},{6,10},{... | collective-permute-start | bytes 98312 | tf_op jit(solution)/shard_map/ppermute | solution.py:340
  106.2 6.9 %copy-start.5 = (bf16[64,2048]{1,0:T(8,128)(2,1)}, bf16[64,2048]{1,0:T(8,128)(2,1)S(1)}, u32[]{:S(2)}) copy-start(bf16[64,2048]{1,0:T(8,128)(2,1)S(1)} %collective-permute-done.16.rest_11_) | copy-start | bytes 786436
  106.2 5.6 %collective-permute-start.6 = (bf16[128,128]{1,0:T(8,128)(2,1)}, bf16[128,128]{1,0:T(8,128)(2,1)S(1)}, u32[]{:S(2)}, u32[]{:S(2)}) collective-permute-start(bf16[128,128]{1,0:T(8,128)(2,1)} %get-tuple-element.27.rest_0_), channel_id=1, source_target_pairs={{0,8},{4,12},{8,0},{12,4},{1,9},{5,13},{9,1},{13,5},{2,10},{6,14},... | collective-permute-start | bytes 98312 | tf_op jit(solution)/shard_map/ppermute | solution.py:340
  108.9 4.2 %copy-start.9 = (bf16[128,512]{1,0:T(8,128)(2,1)}, bf16[128,512]{1,0:T(8,128)(2,1)S(1)}, u32[]{:S(2)}) copy-start(bf16[128,512]{1,0:T(8,128)(2,1)S(1)} %collective-permute-done.11.rest_5_) | copy-start | bytes 393220
  108.9 4.1 %collective-permute-start.7 = (bf16[128,128]{1,0:T(8,128)(2,1)}, bf16[128,128]{1,0:T(8,128)(2,1)S(1)}, u32[]{:S(2)}, u32[]{:S(2)}) collective-permute-start(bf16[128,128]{1,0:T(8,128)(2,1)} %get-tuple-element.27.rest_0_), channel_id=1, source_target_pairs={{0,12},{4,0},{8,4},{12,8},{1,13},{5,1},{9,5},{13,9},{2,14},{6,2},{... | collective-permute-start | bytes 98312 | tf_op jit(solution)/shard_map/ppermute | solution.py:340
  111.1 2.0 %copy-start.7 = (bf16[128,512]{1,0:T(8,128)(2,1)}, bf16[128,512]{1,0:T(8,128)(2,1)S(1)}, u32[]{:S(2)}) copy-start(bf16[128,512]{1,0:T(8,128)(2,1)S(1)} %collective-permute-done.12.rest_6_) | copy-start | bytes 393220
  111.1 2.0 %copy-start.8 = (bf16[128,512]{1,0:T(8,128)(2,1)}, bf16[128,512]{1,0:T(8,128)(2,1)S(1)}, u32[]{:S(2)}) copy-start(bf16[128,512]{1,0:T(8,128)(2,1)S(1)} %collective-permute-done.13.rest_7_) | copy-start | bytes 393220
  111.2 2.0 %copy-start.17 = (bf16[128,128]{1,0:T(8,128)(2,1)}, bf16[128,128]{1,0:T(8,128)(2,1)S(1)}, u32[]{:S(2)}) copy-start(bf16[128,128]{1,0:T(8,128)(2,1)S(1)} %collective-permute-done.5.rest_1_) | copy-start | bytes 98308
  111.8 1.3 copy-start.18
  113.0 0.6 copy-start.19
Sparse Core Ops, SparseCore 0:
  10.2 62.6 all-gather.1

commit v2 on v1

--- a/solution.py
+++ b/solution.py
@@ -19,8 +19,7 @@
 F32 = jnp.float32
 VMEM_LIMIT = 56 * 2**20
 
-SEQ, HALF, PARITY, TENSOR = 0, 1, 2, 3
-ROW_OWN, HAS_OWN, ROW_MATE, HAS_MATE = 4, 6, 8, 10
+SEQ, HALF, PARITY, TENSOR, OWN_ADAPTERS = 0, 1, 2, 3, 4
 
 
 def prep_kernel(where, hidden_ref, weight_ref, *rest):
@@ -165,59 +164,49 @@
     )(where, queries, cache_rows)
 
 
-def rank_kernel(where, hidden_ref, mate_ref, own_maps, mate_maps, own_out, mate_out):
-    r = pl.program_id(0)
+def rank_kernel(where, hidden_ref, maps, mine, others, held, sem):
     depth = hidden_ref.shape[1]
-    for rows, maps, out, flag in (
-        (hidden_ref, own_maps, own_out, HAS_OWN),
-        (mate_ref, mate_maps, mate_out, HAS_MATE),
-    ):
-        here = where[flag + r] == 1
-        part = jnp.dot(rows[...], maps[0, :depth], preferred_element_type=F32).astype(BF)
-        out[0, :NEW_TOK] = jnp.where(here, part, jnp.zeros_like(part))
-        up = maps[0, depth:]
-        out[0, NEW_TOK:] = jnp.where(here, up, jnp.zeros_like(up))
-
-
-def rank_parts(where, hidden, hidden_mate, maps):
-    tokens, depth = hidden.shape
+    copies = [
+        pltpu.make_async_copy(maps.at[where[OWN_ADAPTERS + r]], held.at[r], sem.at[r])
+        for r in range(2)
+    ]
+    for copy in copies:
+        copy.start()
+    parts = []
+    for r in range(2):
+        copies[r].wait()
+        parts.append(
+            jnp.dot(
+                hidden_ref[r * NEW_TOK : (r + 1) * NEW_TOK],
+                held[r, :depth],
+                preferred_element_type=F32,
+            ).astype(BF)
+        )
+    second = where[HALF] == 1
+    ups = [held[r, depth:] for r in range(2)]
+    mine[:NEW_TOK] = jnp.where(second, parts[1], parts[0])
+    mine[NEW_TOK:] = jnp.where(second, ups[1], ups[0])
+    others[:NEW_TOK] = jnp.where(second, parts[0], parts[1])
+    others[NEW_TOK:] = jnp.where(second, ups[0], ups[1])
+
+
+def rank_parts(where, hidden, maps):
     height = maps.shape[1]
-    out = jax.ShapeDtypeStruct((2, NEW_TOK + height - depth, WIDTH), BF)
-    out_spec = pl.BlockSpec((1,) + out.shape[1:], lambda r, w: (r, 0, 0))
+    out = jax.ShapeDtypeStruct((NEW_TOK + height - hidden.shape[1], WIDTH), BF)
+    whole = pl.BlockSpec(memory_space=pltpu.VMEM)
     return pl.pallas_call(
         rank_kernel,
-        grid_spec=pltpu.PrefetchScalarGridSpec(
-            num_scalar_prefetch=1,
-            grid=(2,),
-            in_specs=[
-                pl.BlockSpec((NEW_TOK, depth), lambda r, w: (r, 0)),
-                pl.BlockSpec((NEW_TOK, depth), lambda r, w: (r, 0)),
-                pl.BlockSpec((1, height, WIDTH), lambda r, w: (w[ROW_OWN + r], 0, 0)),
-                pl.BlockSpec((1, height, WIDTH), lambda r, w: (w[ROW_MATE + r], 0, 0)),
-            ],
-            out_specs=[out_spec, out_spec],
-        ),
-        out_shape=[out, out],
-        name="rank_partial",
-    )(where, hidden, hidden_mate, maps, maps)
-
-
-def pair_kernel(where, own_ref, got_ref, mine, others):
-    half = where[HALF]
-    mine[...] = own_ref[half] + got_ref[half]
-    others[...] = own_ref[1 - half] + got_ref[1 - half]
-
-
-def pair_sum(where, own, got):
-    out = jax.ShapeDtypeStruct(own.shape[1:], BF)
-    whole = pl.BlockSpec(memory_space=pltpu.VMEM)
-    return pl.pallas_call(
-        pair_kernel,
-        in_specs=[pl.BlockSpec(memory_space=pltpu.SMEM), whole, whole],
+        in_specs=[
+            pl.BlockSpec(memory_space=pltpu.SMEM),
+            whole,
+            pl.BlockSpec(memory_space=pl.ANY),
+        ],
         out_specs=[whole, whole],
         out_shape=[out, out],
-        name="core_sum",
-    )(where, own, got)
+        scratch_shapes=[pltpu.VMEM((2, height, WIDTH), BF), pltpu.SemaphoreType.DMA((2,))],
+        compiler_params=pltpu.CompilerParams(vmem_limit_bytes=VMEM_LIMIT),
+        name="rank_partial",
+    )(where, hidden, maps)
 
 
 def seq_kernel(where, own, one, two, three, rank_out, up_out):
@@ -243,13 +232,42 @@
     )(where, own, *got)
 
 
-def final_kernel(where, q_ref, cos_ref, sin_ref, up_ref, *rest):
-    ranks, bases, means, logs = rest[:4], rest[4:8], rest[8:12], rest[12:16]
-    kv_out, attention_out, wide = rest[16:]
+def merge_kernel(*refs):
+    means, logs, mean_out, log_out = refs[:4], refs[4:8], refs[8], refs[9]
+    half = means[0].shape[0]
+    tops = [l[...] for l in logs]
+    top = functools.reduce(jnp.maximum, tops)
+    weights = [jnp.exp2(l - top) for l in tops]
+    total = sum(weights)
+    merged = top + jnp.log2(total)
+    weights = [w / total for w in weights]
+    for n in range(16):
+        rows = slice(n * half, (n + 1) * half)
+        cols = slice(n * WIDTH, (n + 1) * WIDTH)
+        mean_out[rows] = sum(
+            w[:, n : n + 1] * m[:, cols].astype(F32) for w, m in zip(weights, means)
+        )
+        log_out[rows] = jnp.broadcast_to(merged[:, n : n + 1], (half, WIDTH))
+
+
+def merge(means, logs):
+    out = jax.ShapeDtypeStruct((16 * means[0].shape[0], WIDTH), F32)
+    whole = pl.BlockSpec(memory_space=pltpu.VMEM)
+    return pl.pallas_call(
+        merge_kernel,
+        in_specs=[whole] * 8,
+        out_specs=[whole, whole],
+        out_shape=[out, out],
+        compiler_params=pltpu.CompilerParams(vmem_limit_bytes=VMEM_LIMIT),
+        name="merge_prefix",
+    )(*means, *logs)
+
+
+def final_kernel(where, q_ref, cos_ref, sin_ref, up_ref, mean_ref, log_ref, base_ref, *rest):
+    ranks, (kv_out, attention_out, wide) = rest[:4], rest[4:]
     half = q_ref.shape[0]
     start = pl.multiple_of(where[PARITY] * half, half)
     rank = sum(r[...].astype(F32) for r in ranks).astype(BF)
-    base = sum(b[...].astype(F32) for b in bases)
     keys, values = [], []
     for h in range(2):
         for e in range(2):
@@ -257,47 +275,44 @@
                 rank[:, e * 64 : (e + 1) * 64], up_ref[2 * e + h], preferred_element_type=F32
             )
             part = 2 * h + e
-            field = base[:, part * WIDTH : (part + 1) * WIDTH] + delta
+            field = base_ref[:, part * WIDTH : (part + 1) * WIDTH] + delta
             if e == 0:
                 field = field * cos_ref[...] + pltpu.roll(field, WIDTH // 2, 1) * sin_ref[...]
             wide[pl.ds(part, NEW_TOK, stride=4), :] = field
             (keys, values)[e].append(field.astype(BF))
     kv_out[...] = wide[pl.ds(start * 4, half * 4), :].astype(BF)
-    row = lax.broadcasted_iota(jnp.int32, (half, NEW_TOK), 0) + start
-    seen = lax.broadcasted_iota(jnp.int32, (half, NEW_TOK), 1) <= row
-    old_logs = [l[...] for l in logs]
+    rows = 8 * half
+    token = lax.broadcasted_iota(jnp.int32, (rows, NEW_TOK), 0) % half + start
+    seen = lax.broadcasted_iota(jnp.int32, (rows, NEW_TOK), 1) <= token
+    ones = jnp.ones((NEW_TOK, WIDTH), BF)
     for h in range(2):
+        q = jnp.concatenate(
+            [q_ref[:, n * WIDTH : (n + 1) * WIDTH] for n in range(h * 8, h * 8 + 8)], axis=0
+        )
+        s = lax.dot_general(q, keys[h], (((1,), (1,)), ((), ())), preferred_element_type=F32)
+        s = jnp.where(seen, s * SCALE, LOW)
+        block = slice(h * rows, (h + 1) * rows)
+        log = log_ref[block]
+        top = jnp.maximum(log, jnp.max(s, axis=1, keepdims=True))
+        weight = jnp.exp2(log - top)
+        p = jnp.exp2(s - top).astype(BF)
+        value = jnp.dot(
+            p, jnp.concatenate([values[h], ones], axis=1), preferred_element_type=F32
+        )
+        out = (value[:, :WIDTH] + weight * mean_ref[block]) / (value[:, WIDTH:] + weight)
+        out = out.astype(BF)
         for j in range(8):
             n = h * 8 + j
-            cols = slice(n * WIDTH, (n + 1) * WIDTH)
-            s = (
-                lax.dot_general(
-                    q_ref[:, cols], keys[h], (((1,), (1,)), ((), ())), preferred_element_type=F32
-                )
-                * SCALE
-            )
-            s = jnp.where(seen, s, LOW)
-            top = jnp.max(s, axis=1, keepdims=True)
-            log = [l[:, n : n + 1] for l in old_logs]
-            for l in log:
-                top = jnp.maximum(top, l)
-            p = jnp.exp2(s - top)
-            total = jnp.sum(p, axis=1, keepdims=True)
-            value = jnp.dot(p.astype(BF), values[h], preferred_element_type=F32)
-            for l, mean in zip(log, means):
-                weight = jnp.exp2(l - top)
-                total += weight
-                value += weight * mean[:, cols].astype(F32)
-            attention_out[:, cols] = (value / total).astype(BF)
-
-
-def final(where, queries, cos, sin, up, ranks, bases, means, logs):
-    half, width = means[0].shape
+            attention_out[:, n * WIDTH : (n + 1) * WIDTH] = out[j * half : (j + 1) * half]
+
+
+def final(where, queries, cos, sin, up, mean, log, base, ranks):
+    half, width = NEW_TOK // 2, queries.shape[1]
 
     def whole(a):
         return pl.BlockSpec(a.shape, lambda i, w: (0,) * a.ndim)
 
-    rest = [cos, sin, up, *ranks, *bases, *means, *logs]
+    rest = [cos, sin, up, mean, log, base, *ranks]
     return pl.pallas_call(
         final_kernel,
         grid_spec=pltpu.PrefetchScalarGridSpec(
@@ -316,7 +331,7 @@
             jax.ShapeDtypeStruct((half, width), BF),
         ],
         compiler_params=pltpu.CompilerParams(vmem_limit_bytes=VMEM_LIMIT),
-        name="new_kv_and_merge",
+        name="new_kv_and_attention",
     )(where, queries, *rest)
 
 
@@ -350,23 +365,10 @@
     request_adapter,
 ):
     seq, group, tensor = (lax.axis_index(a) for a in ("seq", "group", "tensor"))
-    core = group % 2
-    own_adapter = lax.dynamic_slice_in_dim(request_adapter, 2 * group, 2)
-    mate_adapter = lax.dynamic_slice_in_dim(request_adapter, 2 * (group ^ 1), 2)
-
-    def row(adapter):
-        return adapter // 8 * 4 + adapter % 4
-
-    def here(adapter):
-        return (adapter // 4 % 2 == core).astype(jnp.int32)
-
     where = jnp.concatenate(
         [
             jnp.stack([seq, seq // 2, seq % 2, tensor]).astype(jnp.int32),
-            row(own_adapter),
-            here(own_adapter),
-            row(mate_adapter),
-            here(mate_adapter),
+            lax.dynamic_slice_in_dim(request_adapter, 2 * group, 2),
         ]
     )
 
@@ -374,9 +376,7 @@
         adapter_up_weight, (0, seq // 2, 0, seq % 2 * WIDTH), (4, 1, 64, WIDTH)
     )
     maps = jnp.concatenate([adapter_down_weight, quarter[:, 0]], axis=1)
-    same_core = [list(range(c, lax.axis_size("group"), 2)) for c in range(2)]
-    maps = lax.all_gather(maps, "group", axis_index_groups=same_core, axis=0, tiled=True)
-    hidden_mate = flip("group", 1)(hidden)
+    maps = lax.all_gather(maps, "group", axis=0, tiled=True)
 
     parts = prep(where, hidden, key_value_weight.reshape(-1, WIDTH))
     base = parts[0].astype(F32)
@@ -385,28 +385,27 @@
     base = base.astype(BF)
     base_own = lax.dynamic_slice_in_dim(base, seq // 2 * NEW_TOK, NEW_TOK, 0)
     base_other = lax.dynamic_slice_in_dim(base, (1 - seq // 2) * NEW_TOK, NEW_TOK, 0)
-    bases = [
-        base_own,
-        flip("seq", 1)(base_own),
-        flip("seq", 2)(base_other),
-        flip("seq", 3)(base_other),
-    ]
+    base = base_own.astype(F32) + flip("seq", 1)(base_own).astype(F32)
+    base += flip("seq", 2)(base_other).astype(F32) + flip("seq", 3)(base_other).astype(F32)
 
     cache_rows = key_value_cache.reshape(-1, WIDTH)
     o2, o3, l2, l3 = attend(where, queries, cache_rows, True)
     o0, o1, l0, l1 = attend(where, queries, cache_rows, False)
-    means = [o0, flip("seq", 1)(o1), flip("seq", 2)(o2), flip("seq", 3)(o3)]
-    logs = [l0, flip("seq", 1)(l1), flip("seq", 2)(l2), flip("seq", 3)(l3)]
-
-    own, mate = rank_parts(where, hidden, hidden_mate, maps)
-    mine, others = pair_sum(where, own, flip("group", 1)(mate))
+    mean, log = merge(
+        [o0, flip("seq", 1)(o1), flip("seq", 2)(o2), flip("seq", 3)(o3)],
+        [l0, flip("seq", 1)(l1), flip("seq", 2)(l2), flip("seq", 3)(l3)],
+    )
+    cos, sin = rotary_tables()
+
+    maps, mean, log, base, cos, sin = lax.optimization_barrier((maps, mean, log, base, cos, sin))
+
+    mine, others = rank_parts(where, hidden, maps)
     rank, up = seq_sum(
         where, mine, [flip("seq", 1)(mine), flip("seq", 2)(others), flip("seq", 3)(others)]
     )
     ranks = [rank] + [shift("tensor", step)(rank) for step in (1, 2, 3)]
 
-    cos, sin = rotary_tables()
-    new_kv, attention = final(where, queries, cos, sin, up, ranks, bases, means, logs)
+    new_kv, attention = final(where, queries, cos, sin, up, mean, log, base, ranks)
     return new_kv.reshape(-1, 2, 2, WIDTH), attention
 
 

time: 130 us -> 117 us (0.900)
  the two profiles are of different devices: /device:TPU:8 before, /device:TPU:32 now
where the time goes in v2:
time: 117 us; the launch traced here: 116 us
  Pallas kernels  50.9 us (44%)
  starting transfers between devices  28.1 us (24%)
  waiting for transfers between devices  14.2 us (12%)
  between operations  14.2 us (12%)
  local copies, waits for them, and re-layouts  4.26 us (4%)
  other arithmetic  3.9 us (3%)
    pallas_call x2, Pallas kernels, attend(): pl.pallas_call(attend_kernel, grid_spec=pltpu.PrefetchScalarGridSpec(num_...  34.8 us
    ppermute x12, starting transfers between devices, flip(): lax.ppermute(a, axis, [(i, i ^ mask) for i in range(lax.axis_size(axis))])  19.1 us
    ppermute x12, waiting for transfers between devices, flip(): lax.ppermute(a, axis, [(i, i ^ mask) for i in range(lax.axis_size(axis))])  10.9 us
    ppermute x6, starting transfers between devices, shift(): lax.ppermute(a, axis, [(i, (i + step) % size) for i in range(size)])  8.93 us
    pallas_call x1, Pallas kernels, prep(): pl.pallas_call(prep_kernel, grid_spec=pltpu.PrefetchScalarGridSpec(num_sc...  4.98 us
    pallas_call x1, Pallas kernels, final(): pl.pallas_call(final_kernel, grid_spec=pltpu.PrefetchScalarGridSpec(num_s...  3.81 us
    ppermute x6, waiting for transfers between devices, shift(): lax.ppermute(a, axis, [(i, (i + step) % size) for i in range(size)])  3.31 us
    pallas_call x1, Pallas kernels, merge(): pl.pallas_call(merge_kernel, in_specs=[whole] * 8, out_specs=[whole, whol...  2.98 us
  transfers between devices with their start and end apart: 19, of which 7 were waited for; matrix products, arithmetic and copies ran while one was open for 3% of the time, Pallas kernels for 37%

profile of v2, /device:TPU:32, one launch (start us, length us, event | category | flops | bytes accessed | tf_op | source)
XLA Modules:
  0.0 115.6 jit_solution(1201819633349883498)
XLA Ops:
  7.2 0.0 copy-start
  7.2 0.0 all-gather.2.cloned.1.call-start
  7.3 0.9 copy-done
  8.1 1.9 %pad_maximum_fusion = bf16[4,576,128]{2,1,0:T(8,128)(2,1)} fusion(bf16[4,64,128]{2,1,0:T(8,128)(2,1)S(1)} %dynamic-slice_bitcast_fusion, bf16[4,512,128]{2,1,0:T(8,128)(2,1)} %param.9), kind=kLoop, calls=%fused_computation | loop fusion | flops 1179648 | bytes 1179648 | tf_op jit(solution)/shard_map/concatenate | solution.py:378
  10.1 0.0 all-gather.2.cloned.1.call-update
  10.1 0.7 dynamic_slice.12
  10.8 0.7 concatenate.12.where
  11.5 5.0 %base_partial.1 = (bf16[256,512]{1,0:T(8,128)(2,1)}, bf16[256,512]{1,0:T(8,128)(2,1)}, bf16[256,512]{1,0:T(8,128)(2,1)}, bf16[256,512]{1,0:T(8,128)(2,1)}) custom-call(s32[6]{0:T(128)} %concatenate.12.where, bf16[256,512]{1,0:T(8,128)(2,1)} %hidden_ref.3, bf16[8192,128]{1,0:T(8,128)(2,1)} %bitcast.11), custom_call_target="tpu_custom_call" | custom-call | flops 2147483648 | bytes 4194304 | tf_op jit(solution)/shard_map/base_partial/pallas_call | solution.py:42
  16.5 1.5 %collective-permute-start.6 = (bf16[256,512]{1,0:T(8,128)(2,1)}, bf16[256,512]{1,0:T(8,128)(2,1)S(1)}, u32[]{:S(2)}, u32[]{:S(2)}) collective-permute-start(bf16[256,512]{1,0:T(8,128)(2,1)} %get-tuple-element.39), channel_id=1, source_target_pairs={{0,4},{4,8},{8,12},{12,0},{1,5},{5,9},{9,13},{13,1},{2,6},{6,10},{... | collective-permute-start | bytes 786440 | tf_op jit(solution)/shard_map/ppermute | solution.py:355
  18.0 2.8 %collective-permute-start.7 = (bf16[256,512]{1,0:T(8,128)(2,1)}, bf16[256,512]{1,0:T(8,128)(2,1)S(1)}, u32[]{:S(2)}, u32[]{:S(2)}) collective-permute-start(bf16[256,512]{1,0:T(8,128)(2,1)} %get-tuple-element.40), channel_id=1, source_target_pairs={{0,8},{4,12},{8,0},{12,4},{1,9},{5,13},{9,1},{13,5},{2,10},{6,14},... | collective-permute-start | bytes 786440 | tf_op jit(solution)/shard_map/ppermute | solution.py:355
  20.7 1.4 %collective-permute-start.8 = (bf16[256,512]{1,0:T(8,128)(2,1)}, bf16[256,512]{1,0:T(8,128)(2,1)S(1)}, u32[]{:S(2)}, u32[]{:S(2)}) collective-permute-start(bf16[256,512]{1,0:T(8,128)(2,1)} %get-tuple-element.41), channel_id=1, source_target_pairs={{0,12},{4,0},{8,4},{12,8},{1,13},{5,1},{9,5},{13,9},{2,14},{6,2},{... | collective-permute-start | bytes 786440 | tf_op jit(solution)/shard_map/ppermute | solution.py:355
  22.2 17.3 %attend_own.1 = (bf16[64,2048]{1,0:T(8,128)(2,1)}, bf16[64,2048]{1,0:T(8,128)(2,1)}, f32[64,128]{1,0:T(8,128)}, f32[64,128]{1,0:T(8,128)}) custom-call(s32[6]{0:T(128)} %concatenate.12.where, bf16[256,2048]{1,0:T(8,128)(2,1)} %q_ref.5, bf16[32768,128]{1,0:T(8,128)(2,1)} %bitcast.9), custom_call_target="tpu_custom_call" | custom-call | flops 8589934592 | bytes 5242880 | tf_op jit(solution)/shard_map/attend_own/pallas_call | solution.py:139
  39.5 1.9 %collective-permute-start = (bf16[64,2048]{1,0:T(8,128)(2,1)}, bf16[64,2048]{1,0:T(8,128)(2,1)S(1)}, u32[]{:S(2)}, u32[]{:S(2)}) collective-permute-start(bf16[64,2048]{1,0:T(8,128)(2,1)} %get-tuple-element.29), channel_id=1, source_target_pairs={{0,1},{1,0},{2,3},{3,2},{4,5},{5,4},{6,7},{7,6},{8,9},{9,8},{10,11... | collective-permute-start | bytes 786440 | tf_op jit(solution)/shard_map/ppermute | solution.py:348
  41.4 17.4 %attend_other.1 = (bf16[64,2048]{1,0:T(8,128)(2,1)}, bf16[64,2048]{1,0:T(8,128)(2,1)}, f32[64,128]{1,0:T(8,128)}, f32[64,128]{1,0:T(8,128)}) custom-call(s32[6]{0:T(128)} %concatenate.12.where, bf16[256,2048]{1,0:T(8,128)(2,1)} %q_ref.5, bf16[32768,128]{1,0:T(8,128)(2,1)} %bitcast.10), custom_call_target="tpu_custom_call" | custom-call | flops 8589934592 | bytes 5242880 | tf_op jit(solution)/shard_map/attend_other/pallas_call | solution.py:139
  58.8 3.1 %collective-permute-start.1 = (bf16[64,2048]{1,0:T(8,128)(2,1)}, bf16[64,2048]{1,0:T(8,128)(2,1)S(1)}, u32[]{:S(2)}, u32[]{:S(2)}) collective-permute-start(bf16[64,2048]{1,0:T(8,128)(2,1)} %get-tuple-element.30), channel_id=1, source_target_pairs={{0,2},{1,3},{2,0},{3,1},{4,6},{5,7},{6,4},{7,5},{8,10},{9,11},{10,... | collective-permute-start | bytes 786440 | tf_op jit(solution)/shard_map/ppermute | solution.py:348
  61.9 0.0 collective-permute-done.6
  62.0 0.0 copy-done.14
  62.0 0.1 collective-permute-start.3
  62.1 0.0 collective-permute-done.7
  62.1 1.4 %collective-permute-start.4 = (f32[64,128]{1,0:T(8,128)}, f32[64,128]{1,0:T(8,128)S(1)}, u32[]{:S(2)}, u32[]{:S(2)}) collective-permute-start(f32[64,128]{1,0:T(8,128)} %get-tuple-element.34), channel_id=1, source_target_pairs={{0,2},{1,3},{2,0},{3,1},{4,6},{5,7},{6,4},{7,5},{8,10},{9,11},{10,... | collective-permute-start | bytes 98312 | tf_op jit(solution)/shard_map/ppermute | solution.py:348
  63.5 0.0 collective-permute-done.8
  63.5 3.3 %collective-permute-start.5 = (f32[64,128]{1,0:T(8,128)}, f32[64,128]{1,0:T(8,128)S(1)}, u32[]{:S(2)}, u32[]{:S(2)}) collective-permute-start(f32[64,128]{1,0:T(8,128)} %get-tuple-element.35), channel_id=1, source_target_pairs={{0,3},{1,2},{2,1},{3,0},{4,7},{5,6},{6,5},{7,4},{8,11},{9,10},{10,... | collective-permute-start | bytes 98312 | tf_op jit(solution)/shard_map/ppermute | solution.py:348
  66.8 0.0 copy-done.1
  66.8 0.1 add_convert_fusion
  66.9 1.1 collective-permute-done.3.refs_5_
  68.1 1.0 collective-permute-start.2
  69.1 0.0 collective-permute-done.4.refs_6_
  69.1 2.9 %collective-permute-start.10 = (bf16[128,512]{1,0:T(8,128)(2,1)S(1)}, bf16[128,512]{1,0:T(8,128)(2,1)S(1)}, u32[]{:S(2)}, u32[]{:S(2)}) collective-permute-start(bf16[128,512]{1,0:T(8,128)(2,1)S(1)} %get-tuple-element.55), channel_id=1, source_target_pairs={{0,2},{1,3},{2,0},{3,1},{4,6},{5,7},{6,4},{7,5},{8,10},{9,11},{10,... | collective-permute-start | bytes 393224 | tf_op jit(solution)/shard_map/ppermute | solution.py:348
  72.0 0.0 collective-permute-done.5.refs_7_
  72.0 0.7 collective-permute-start.11
  72.7 0.0 collective-permute-done.refs_1_
  72.7 0.0 collective-permute-start.9
  72.7 0.3 fusion
  73.0 0.8 pad_maximum_fusion.1
  73.8 0.0 collective-permute-done.1.refs_2_
  73.8 5.6 %collective-permute-done.2.refs_3_ = bf16[64,2048]{1,0:T(8,128)(2,1)S(1)} collective-permute-done((bf16[64,2048]{1,0:T(8,128)(2,1)}, bf16[64,2048]{1,0:T(8,128)(2,1)S(1)}, u32[]{:S(2)}, u32[]{:S(2)}) %collective-permute-start.2) | collective-permute-done | bytes 262176 | tf_op jit(solution)/shard_map/ppermute | solution.py:348
  79.3 0.0 copy-done.12
  79.3 0.0 copy-done.2
  79.3 0.0 copy-done.3
  79.3 0.7 copy-done.4
  80.0 3.0 %merge_prefix.1 = (f32[1024,128]{1,0:T(8,128)}, f32[1024,128]{1,0:T(8,128)}) custom-call(bf16[64,2048]{1,0:T(8,128)(2,1)} %get-tuple-element.28.refs_0_, bf16[64,2048]{1,0:T(8,128)(2,1)} %copy-done.2, bf16[64,2048]{1,0:T(8,128)(2,1)} %copy-done.3, bf16[64,2048]{1,0:T(8,128)(2,1)} %copy-done.4, f32[64,128]{1,0:T(8,128)} %get-tuple-element.32.refs_4_, ...), custom_call_target="tpu_custom_call" | custom-call | tf_op jit(solution)/shard_map/merge_prefix/pallas_call | solution.py:256
  83.0 0.0 collective-permute-done.10
  83.0 0.0 collective-permute-done.11
  83.0 0.0 collective-permute-done.9
  83.0 0.8 add_add_fusion.base_ref
  83.8 2.9 %rank_partial.1 = (bf16[192,128]{1,0:T(8,128)(2,1)}, bf16[192,128]{1,0:T(8,128)(2,1)}) custom-call(s32[6]{0:T(128)} %concatenate.12.where, bf16[256,512]{1,0:T(8,128)(2,1)} %hidden_ref.3, bf16[64,576,128]{2,1,0:T(8,128)(2,1)} %all-gather.2.cloned.1.call-done.maps), custom_call_target="tpu_custom_call" | custom-call | tf_op jit(solution)/shard_map/rank_partial/pallas_call | solution.py:197
  86.7 0.6 collective-permute-start.12
  87.3 2.8 %collective-permute-start.13 = (bf16[192,128]{1,0:T(8,128)(2,1)}, bf16[192,128]{1,0:T(8,128)(2,1)S(1)}, u32[]{:S(2)}, u32[]{:S(2)}) collective-permute-start(bf16[192,128]{1,0:T(8,128)(2,1)} %get-tuple-element.46), channel_id=1, source_target_pairs={{0,2},{1,3},{2,0},{3,1},{4,6},{5,7},{6,4},{7,5},{8,10},{9,11},{10,... | collective-permute-start | bytes 147464 | tf_op jit(solution)/shard_map/ppermute | solution.py:348
  90.1 1.3 %collective-permute-start.14 = (bf16[192,128]{1,0:T(8,128)(2,1)}, bf16[192,128]{1,0:T(8,128)(2,1)S(1)}, u32[]{:S(2)}, u32[]{:S(2)}) collective-permute-start(bf16[192,128]{1,0:T(8,128)(2,1)} %get-tuple-element.46), channel_id=1, source_target_pairs={{0,3},{1,2},{2,1},{3,0},{4,7},{5,6},{6,5},{7,4},{8,11},{9,10},{10,... | collective-permute-start | bytes 147464 | tf_op jit(solution)/shard_map/ppermute | solution.py:348
  91.5 0.0 collective-permute-done.12.one
  91.5 1.6 %collective-permute-done.13.two = bf16[192,128]{1,0:T(8,128)(2,1)S(1)} collective-permute-done((bf16[192,128]{1,0:T(8,128)(2,1)}, bf16[192,128]{1,0:T(8,128)(2,1)S(1)}, u32[]{:S(2)}, u32[]{:S(2)}) %collective-permute-start.13) | collective-permute-done | bytes 49184 | tf_op jit(solution)/shard_map/ppermute | solution.py:348
  93.1 2.5 %collective-permute-done.14.three = bf16[192,128]{1,0:T(8,128)(2,1)S(1)} collective-permute-done((bf16[192,128]{1,0:T(8,128)(2,1)}, bf16[192,128]{1,0:T(8,128)(2,1)S(1)}, u32[]{:S(2)}, u32[]{:S(2)}) %collective-permute-start.14) | collective-permute-done | bytes 49184 | tf_op jit(solution)/shard_map/ppermute | solution.py:348
  95.6 0.0 copy-done.6
  95.6 0.6 copy-done.7
  96.3 1.5 %seq_sum.1 = (bf16[128,128]{1,0:T(8,128)(2,1)}, bf16[4,64,128]{2,1,0:T(8,128)(2,1)}) custom-call(s32[6]{0:T(128)} %concatenate.12.where, bf16[192,128]{1,0:T(8,128)(2,1)} %get-tuple-element.45.own, bf16[192,128]{1,0:T(8,128)(2,1)} %copy-done.5, bf16[192,128]{1,0:T(8,128)(2,1)} %copy-done.6, bf16[192,128]{1,0:T(8,128)(2,1)} %copy-done.7), custom_call_target="tpu_custom_call" | custom-call | tf_op jit(solution)/shard_map/seq_sum/pallas_call | solution.py:223
  97.8 0.6 collective-permute-start.15
  98.4 1.2 %collective-permute-start.16 = (bf16[128,128]{1,0:T(8,128)(2,1)}, bf16[128,128]{1,0:T(8,128)(2,1)S(1)}, u32[]{:S(2)}, u32[]{:S(2)}) collective-permute-start(bf16[128,128]{1,0:T(8,128)(2,1)} %get-tuple-element.51.rest_0_), channel_id=1, source_target_pairs={{0,8},{4,12},{8,0},{12,4},{1,9},{5,13},{9,1},{13,5},{2,10},{6,14},... | collective-permute-start | bytes 98312 | tf_op jit(solution)/shard_map/ppermute | solution.py:355
  99.5 1.5 %collective-permute-start.17 = (bf16[128,128]{1,0:T(8,128)(2,1)}, bf16[128,128]{1,0:T(8,128)(2,1)S(1)}, u32[]{:S(2)}, u32[]{:S(2)}) collective-permute-start(bf16[128,128]{1,0:T(8,128)(2,1)} %get-tuple-element.51.rest_0_), channel_id=1, source_target_pairs={{0,12},{4,0},{8,4},{12,8},{1,13},{5,1},{9,5},{13,9},{2,14},{6,2},{... | collective-permute-start | bytes 98312 | tf_op jit(solution)/shard_map/ppermute | solution.py:355
  101.0 2.1 %collective-permute-done.15.rest_1_ = bf16[128,128]{1,0:T(8,128)(2,1)S(1)} collective-permute-done((bf16[128,128]{1,0:T(8,128)(2,1)}, bf16[128,128]{1,0:T(8,128)(2,1)S(1)}, u32[]{:S(2)}, u32[]{:S(2)}) %collective-permute-start.15) | collective-permute-done | bytes 32800 | tf_op jit(solution)/shard_map/ppermute | solution.py:355
  103.1 0.8 collective-permute-done.16.rest_2_
  104.0 0.4 collective-permute-done.17.rest_3_
  104.3 0.2 copy-done.9
  104.6 0.4 copy-done.10
  105.0 3.8 %new_kv_and_attention.1 = (bf16[256,128]{1,0:T(8,128)(2,1)}, bf16[64,2048]{1,0:T(8,128)(2,1)}) custom-call(s32[6]{0:T(128)} %concatenate.12.where, bf16[256,2048]{1,0:T(8,128)(2,1)} %q_ref.5, f32[128,128]{1,0:T(8,128)} %get-tuple-element.42.cos_ref, f32[128,128]{1,0:T(8,128)} %get-tuple-element.43.sin_ref, bf16[4,64,128]{2,1,0:T(8,128)(2,1)} %get-tuple-element.47.up_ref, ...), custom_call_target="tpu_custom_call" | custom-call | tf_op jit(solution)/shard_map/new_kv_and_attention/pallas_call | solution.py:316
  (23 shorter events, 0.1 us)
Async XLA Ops:
  7.2 1.0 copy-start
  7.2 76.6 %all-gather.2.cloned.1.call-start = ((), (), s32[]{:S(2)}) async-start(), calls=%async_computation | async-start | bytes 10027008 | tf_op jit(solution)/shard_map/all_gather | solution.py:379
  16.5 45.5 %collective-permute-start.6 = (bf16[256,512]{1,0:T(8,128)(2,1)}, bf16[256,512]{1,0:T(8,128)(2,1)S(1)}, u32[]{:S(2)}, u32[]{:S(2)}) collective-permute-start(bf16[256,512]{1,0:T(8,128)(2,1)} %get-tuple-element.39), channel_id=1, source_target_pairs={{0,4},{4,8},{8,12},{12,0},{1,5},{5,9},{9,13},{13,1},{2,6},{6,10},{... | collective-permute-start | bytes 786440 | tf_op jit(solution)/shard_map/ppermute | solution.py:355
  18.0 44.1 %collective-permute-start.7 = (bf16[256,512]{1,0:T(8,128)(2,1)}, bf16[256,512]{1,0:T(8,128)(2,1)S(1)}, u32[]{:S(2)}, u32[]{:S(2)}) collective-permute-start(bf16[256,512]{1,0:T(8,128)(2,1)} %get-tuple-element.40), channel_id=1, source_target_pairs={{0,8},{4,12},{8,0},{12,4},{1,9},{5,13},{9,1},{13,5},{2,10},{6,14},... | collective-permute-start | bytes 786440 | tf_op jit(solution)/shard_map/ppermute | solution.py:355
  20.7 42.8 %collective-permute-start.8 = (bf16[256,512]{1,0:T(8,128)(2,1)}, bf16[256,512]{1,0:T(8,128)(2,1)S(1)}, u32[]{:S(2)}, u32[]{:S(2)}) collective-permute-start(bf16[256,512]{1,0:T(8,128)(2,1)} %get-tuple-element.41), channel_id=1, source_target_pairs={{0,12},{4,0},{8,4},{12,8},{1,13},{5,1},{9,5},{13,9},{2,14},{6,2},{... | collective-permute-start | bytes 786440 | tf_op jit(solution)/shard_map/ppermute | solution.py:355
  39.5 22.4 %copy-start.14 = (f32[64,128]{1,0:T(8,128)S(1)}, f32[64,128]{1,0:T(8,128)}, u32[]{:S(2)}) copy-start(f32[64,128]{1,0:T(8,128)} %get-tuple-element.33) | copy-start | bytes 98308
  39.5 27.2 %copy-start.1 = (bf16[256,512]{1,0:T(8,128)(2,1)S(1)}, bf16[256,512]{1,0:T(8,128)(2,1)}, u32[]{:S(2)}) copy-start(bf16[256,512]{1,0:T(8,128)(2,1)} %get-tuple-element.38) | copy-start | bytes 786436
  39.5 33.1 %collective-permute-start = (bf16[64,2048]{1,0:T(8,128)(2,1)}, bf16[64,2048]{1,0:T(8,128)(2,1)S(1)}, u32[]{:S(2)}, u32[]{:S(2)}) collective-permute-start(bf16[64,2048]{1,0:T(8,128)(2,1)} %get-tuple-element.29), channel_id=1, source_target_pairs={{0,1},{1,0},{2,3},{3,2},{4,5},{5,4},{6,7},{7,6},{8,9},{9,8},{10,11... | collective-permute-start | bytes 786440 | tf_op jit(solution)/shard_map/ppermute | solution.py:348
  58.8 14.9 %collective-permute-start.1 = (bf16[64,2048]{1,0:T(8,128)(2,1)}, bf16[64,2048]{1,0:T(8,128)(2,1)S(1)}, u32[]{:S(2)}, u32[]{:S(2)}) collective-permute-start(bf16[64,2048]{1,0:T(8,128)(2,1)} %get-tuple-element.30), channel_id=1, source_target_pairs={{0,2},{1,3},{2,0},{3,1},{4,6},{5,7},{6,4},{7,5},{8,10},{9,11},{10,... | collective-permute-start | bytes 786440 | tf_op jit(solution)/shard_map/ppermute | solution.py:348
  62.0 6.1 %collective-permute-start.3 = (f32[64,128]{1,0:T(8,128)S(1)}, f32[64,128]{1,0:T(8,128)S(1)}, u32[]{:S(2)}, u32[]{:S(2)}) collective-permute-start(f32[64,128]{1,0:T(8,128)S(1)} %copy-done.14), channel_id=1, source_target_pairs={{0,1},{1,0},{2,3},{3,2},{4,5},{5,4},{6,7},{7,6},{8,9},{9,8},{10,11... | collective-permute-start | bytes 98312 | tf_op jit(solution)/shard_map/ppermute | solution.py:348
  62.1 7.0 %collective-permute-start.4 = (f32[64,128]{1,0:T(8,128)}, f32[64,128]{1,0:T(8,128)S(1)}, u32[]{:S(2)}, u32[]{:S(2)}) collective-permute-start(f32[64,128]{1,0:T(8,128)} %get-tuple-element.34), channel_id=1, source_target_pairs={{0,2},{1,3},{2,0},{3,1},{4,6},{5,7},{6,4},{7,5},{8,10},{9,11},{10,... | collective-permute-start | bytes 98312 | tf_op jit(solution)/shard_map/ppermute | solution.py:348
  63.5 8.5 %collective-permute-start.5 = (f32[64,128]{1,0:T(8,128)}, f32[64,128]{1,0:T(8,128)S(1)}, u32[]{:S(2)}, u32[]{:S(2)}) collective-permute-start(f32[64,128]{1,0:T(8,128)} %get-tuple-element.35), channel_id=1, source_target_pairs={{0,3},{1,2},{2,1},{3,0},{4,7},{5,6},{6,5},{7,4},{8,11},{9,10},{10,... | collective-permute-start | bytes 98312 | tf_op jit(solution)/shard_map/ppermute | solution.py:348
  68.1 11.3 %copy-start.11 = (f32[64,128]{1,0:T(8,128)}, f32[64,128]{1,0:T(8,128)S(1)}, u32[]{:S(2)}) copy-start(f32[64,128]{1,0:T(8,128)S(1)} %collective-permute-done.3.refs_5_) | copy-start | bytes 98308
  68.1 11.2 %collective-permute-start.2 = (bf16[64,2048]{1,0:T(8,128)(2,1)}, bf16[64,2048]{1,0:T(8,128)(2,1)S(1)}, u32[]{:S(2)}, u32[]{:S(2)}) collective-permute-start(bf16[64,2048]{1,0:T(8,128)(2,1)} %get-tuple-element.31), channel_id=1, source_target_pairs={{0,3},{1,2},{2,1},{3,0},{4,7},{5,6},{6,5},{7,4},{8,11},{9,10},{10,... | collective-permute-start | bytes 786440 | tf_op jit(solution)/shard_map/ppermute | solution.py:348
  69.1 10.2 %copy-start.12 = (f32[64,128]{1,0:T(8,128)}, f32[64,128]{1,0:T(8,128)S(1)}, u32[]{:S(2)}) copy-start(f32[64,128]{1,0:T(8,128)S(1)} %collective-permute-done.4.refs_6_) | copy-start | bytes 98308
  69.1 13.9 %collective-permute-start.10 = (bf16[128,512]{1,0:T(8,128)(2,1)S(1)}, bf16[128,512]{1,0:T(8,128)(2,1)S(1)}, u32[]{:S(2)}, u32[]{:S(2)}) collective-permute-start(bf16[128,512]{1,0:T(8,128)(2,1)S(1)} %get-tuple-element.55), channel_id=1, source_target_pairs={{0,2},{1,3},{2,0},{3,1},{4,6},{5,7},{6,4},{7,5},{8,10},{9,11},{10,... | collective-permute-start | bytes 393224 | tf_op jit(solution)/shard_map/ppermute | solution.py:348
  72.0 7.4 %copy-start.13 = (f32[64,128]{1,0:T(8,128)}, f32[64,128]{1,0:T(8,128)S(1)}, u32[]{:S(2)}) copy-start(f32[64,128]{1,0:T(8,128)S(1)} %collective-permute-done.5.refs_7_) | copy-start | bytes 98308
  72.0 11.0 %collective-permute-start.11 = (bf16[128,512]{1,0:T(8,128)(2,1)S(1)}, bf16[128,512]{1,0:T(8,128)(2,1)S(1)}, u32[]{:S(2)}, u32[]{:S(2)}) collective-permute-start(bf16[128,512]{1,0:T(8,128)(2,1)S(1)} %get-tuple-element.55), channel_id=1, source_target_pairs={{0,3},{1,2},{2,1},{3,0},{4,7},{5,6},{6,5},{7,4},{8,11},{9,10},{10,... | collective-permute-start | bytes 393224 | tf_op jit(solution)/shard_map/ppermute | solution.py:348
  72.7 6.7 %copy-start.2 = (bf16[64,2048]{1,0:T(8,128)(2,1)}, bf16[64,2048]{1,0:T(8,128)(2,1)S(1)}, u32[]{:S(2)}) copy-start(bf16[64,2048]{1,0:T(8,128)(2,1)S(1)} %collective-permute-done.refs_1_) | copy-start | bytes 786436
  72.7 10.3 %collective-permute-start.9 = (bf16[128,512]{1,0:T(8,128)(2,1)S(1)}, bf16[128,512]{1,0:T(8,128)(2,1)S(1)}, u32[]{:S(2)}, u32[]{:S(2)}) collective-permute-start(bf16[128,512]{1,0:T(8,128)(2,1)S(1)} %get-tuple-element.54), channel_id=1, source_target_pairs={{0,1},{1,0},{2,3},{3,2},{4,5},{5,4},{6,7},{7,6},{8,9},{9,8},{10,11... | collective-permute-start | bytes 393224 | tf_op jit(solution)/shard_map/ppermute | solution.py:348
  73.8 5.6 %copy-start.3 = (bf16[64,2048]{1,0:T(8,128)(2,1)}, bf16[64,2048]{1,0:T(8,128)(2,1)S(1)}, u32[]{:S(2)}) copy-start(bf16[64,2048]{1,0:T(8,128)(2,1)S(1)} %collective-permute-done.1.refs_2_) | copy-start | bytes 786436
  79.3 0.7 copy-start.4
  86.7 4.8 %collective-permute-start.12 = (bf16[192,128]{1,0:T(8,128)(2,1)}, bf16[192,128]{1,0:T(8,128)(2,1)S(1)}, u32[]{:S(2)}, u32[]{:S(2)}) collective-permute-start(bf16[192,128]{1,0:T(8,128)(2,1)} %get-tuple-element.45.own), channel_id=1, source_target_pairs={{0,1},{1,0},{2,3},{3,2},{4,5},{5,4},{6,7},{7,6},{8,9},{9,8},{10,11... | collective-permute-start | bytes 147464 | tf_op jit(solution)/shard_map/ppermute | solution.py:348
  87.3 5.8 %collective-permute-start.13 = (bf16[192,128]{1,0:T(8,128)(2,1)}, bf16[192,128]{1,0:T(8,128)(2,1)S(1)}, u32[]{:S(2)}, u32[]{:S(2)}) collective-permute-start(bf16[192,128]{1,0:T(8,128)(2,1)} %get-tuple-element.46), channel_id=1, source_target_pairs={{0,2},{1,3},{2,0},{3,1},{4,6},{5,7},{6,4},{7,5},{8,10},{9,11},{10,... | collective-permute-start | bytes 147464 | tf_op jit(solution)/shard_map/ppermute | solution.py:348
  90.1 5.5 %collective-permute-start.14 = (bf16[192,128]{1,0:T(8,128)(2,1)}, bf16[192,128]{1,0:T(8,128)(2,1)S(1)}, u32[]{:S(2)}, u32[]{:S(2)}) collective-permute-start(bf16[192,128]{1,0:T(8,128)(2,1)} %get-tuple-element.46), channel_id=1, source_target_pairs={{0,3},{1,2},{2,1},{3,0},{4,7},{5,6},{6,5},{7,4},{8,11},{9,10},{10,... | collective-permute-start | bytes 147464 | tf_op jit(solution)/shard_map/ppermute | solution.py:348
  91.5 4.2 %copy-start.5 = (bf16[192,128]{1,0:T(8,128)(2,1)}, bf16[192,128]{1,0:T(8,128)(2,1)S(1)}, u32[]{:S(2)}) copy-start(bf16[192,128]{1,0:T(8,128)(2,1)S(1)} %collective-permute-done.12.one) | copy-start | bytes 147460
  93.1 2.6 %copy-start.6 = (bf16[192,128]{1,0:T(8,128)(2,1)}, bf16[192,128]{1,0:T(8,128)(2,1)S(1)}, u32[]{:S(2)}) copy-start(bf16[192,128]{1,0:T(8,128)(2,1)S(1)} %collective-permute-done.13.two) | copy-start | bytes 147460
  95.6 0.6 copy-start.7
  97.8 5.3 %collective-permute-start.15 = (bf16[128,128]{1,0:T(8,128)(2,1)}, bf16[128,128]{1,0:T(8,128)(2,1)S(1)}, u32[]{:S(2)}, u32[]{:S(2)}) collective-permute-start(bf16[128,128]{1,0:T(8,128)(2,1)} %get-tuple-element.51.rest_0_), channel_id=1, source_target_pairs={{0,4},{4,8},{8,12},{12,0},{1,5},{5,9},{9,13},{13,1},{2,6},{6,10},{... | collective-permute-start | bytes 98312 | tf_op jit(solution)/shard_map/ppermute | solution.py:355
  98.4 5.6 %collective-permute-start.16 = (bf16[128,128]{1,0:T(8,128)(2,1)}, bf16[128,128]{1,0:T(8,128)(2,1)S(1)}, u32[]{:S(2)}, u32[]{:S(2)}) collective-permute-start(bf16[128,128]{1,0:T(8,128)(2,1)} %get-tuple-element.51.rest_0_), channel_id=1, source_target_pairs={{0,8},{4,12},{8,0},{12,4},{1,9},{5,13},{9,1},{13,5},{2,10},{6,14},... | collective-permute-start | bytes 98312 | tf_op jit(solution)/shard_map/ppermute | solution.py:355
  99.5 4.8 %collective-permute-start.17 = (bf16[128,128]{1,0:T(8,128)(2,1)}, bf16[128,128]{1,0:T(8,128)(2,1)S(1)}, u32[]{:S(2)}, u32[]{:S(2)}) collective-permute-start(bf16[128,128]{1,0:T(8,128)(2,1)} %get-tuple-element.51.rest_0_), channel_id=1, source_target_pairs={{0,12},{4,0},{8,4},{12,8},{1,13},{5,1},{9,5},{13,9},{2,14},{6,2},{... | collective-permute-start | bytes 98312 | tf_op jit(solution)/shard_map/ppermute | solution.py:355
  103.1 1.2 %copy-start.8 = (bf16[128,128]{1,0:T(8,128)(2,1)}, bf16[128,128]{1,0:T(8,128)(2,1)S(1)}, u32[]{:S(2)}) copy-start(bf16[128,128]{1,0:T(8,128)(2,1)S(1)} %collective-permute-done.15.rest_1_) | copy-start | bytes 98308
  104.0 0.6 copy-start.9
  104.3 0.6 copy-start.10
Sparse Core Ops, SparseCore 0:
  10.2 61.5 all-gather.1
